TPU v7x, 256 devices: a whole 4x4x8 slice. The times are simulated.
256 devices in a mesh: elem: 64 (over z, y, core), gpt: 4 (over x).
Axes of the slice: x: 4, y: 4, z: 8, core: 2. Of those that a mesh axis runs over, the one named last changes fastest.
Arguments:
- thermal_state: float32 [72, 32768], P(None, 'elem'), may hold values from 0.7 to 1.3
- moisture_content: float32 [72, 32768], P(None, 'elem'), may hold values from 0.01 to 1
- lateral_velocity_components: float32 [2, 72, 32768], P(None, None, 'elem'), may hold values from -6 to 6
- sun_elevation_factor: float32 [32768], P('elem'), may hold values from 0.05 to 1
- surface_albedo_values: float32 [32768], P('elem'), may hold values from 0.1 to 0.9
- turbulent_diffusion_strength: float32 [32768], P('elem'), may hold values from 0.3 to 3
- sunlit_indicator: int32 [32768], P('elem'), may hold values 0 or 1
- destination_partition: int32 [32768, 1], P('elem'), may hold values from 0 to 63; in each aligned block of 512 rows (0 to 511, 512 to 1023, ...) at most 16 rows name the same one
- adjacent_elements: int32 [2048, 4], P('elem'), may hold values from 0 to 2047, as said below
- optical_extinction: float32 [56, 72], P('gpt'), may hold values from 0.002 to 0.05
- insolation_quadrature_share: float32 [56], P('gpt'), may hold values from 0.01 to 0.1
Outputs:
- tendency_out: float32 [4, 72, 32768], P(None, None, 'elem')
- span_heating: float32 [72, 65536], P(None, ('elem', 'gpt'))
Inputs may be any that keep to these rules, and one draw needn't show every extreme that they name: `destination_partition`: among the 512 columns of one device at most 16 have the same span; in every draw some device has exactly 16 columns for one span. `adjacent_elements`: row e lists the elements e - 1, e + 1, e - a and e + b modulo 2048, with a and b from 1 to 32; b equals 32 for every element whose number is a multiple of 32.
All inputs are finite; a program needn't handle non-finite values. No bound on the sum of `sunlit_indicator` on one device may be relied on, other than what follows from the above.
Results may differ from a plain program's by a relative error of at most 0.000098.
Values sent between devices are 32-bit elements; how exact they have to be, the bound alone decides.
No kernel may reach another device: no remote copies, remote signals or barrier semaphores. Data moves between devices by JAX's collectives and lax.ppermute only.
A program may use at most 64 MiB of HBM per device.

v0:
```python
import functools
import math

import jax
import jax.numpy as jnp
from jax import lax
from jax.experimental import pallas as pl
from jax.experimental.pallas import tpu as pltpu
from jax.sharding import PartitionSpec as P

LEVELS = 72
COLS = 512
EPTS = 16
LANES = 128
GROUPS = 7
DIFFUSIVITY = 1.66
SCALE = DIFFUSIVITY * math.log2(math.e)
VMEM = pl.BlockSpec(memory_space=pltpu.VMEM)
AXES = ("elem", "gpt")
BF16 = jnp.bfloat16
F32 = jnp.float32


def iota(shape, dim):
    return lax.broadcasted_iota(jnp.int32, shape, dim)


def split(x):
    high = x.astype(BF16)
    rest = x - high.astype(F32)
    middle = rest.astype(BF16)
    low = (rest - middle.astype(F32)).astype(BF16)
    return jnp.concatenate([high, middle, low], axis=0)


def joined(y):
    rows = y.shape[0] // 3
    return y[:rows] + y[rows : 2 * rows] + y[2 * rows :]


def times(x, table):
    return joined(jnp.dot(split(x), table, preferred_element_type=F32))


def element_mean(field):
    at = field * 32 + (iota((COLS, LANES), 0) >> 4)
    return jnp.where(iota((COLS, LANES), 1) == at, 1.0 / EPTS, 0.0).astype(BF16)


def pack_kernel(t_ref, q_ref, mu_ref, albedo_ref, lit_ref, dest_ref, *outs):
    place = lax.axis_index("elem") & 15
    member = lax.axis_index("gpt")
    dest = dest_ref[...]
    onehot = jnp.where(dest == iota((64, COLS), 0), 1.0, 0.0)
    before = jnp.where(iota((COLS, COLS), 0) < iota((COLS, COLS), 1), 1.0, 0.0).astype(BF16)
    earlier = jnp.dot(onehot.astype(BF16), before, preferred_element_type=F32)
    rank = jnp.sum(onehot * earlier, axis=0, keepdims=True).astype(jnp.int32)
    apart = (dest & 15) ^ place
    slot = (apart & 3) * 64 + (apart >> 2) * 16 + rank
    sent = ((dest >> 4) == member) & (lit_ref[...] != 0)
    slot = jnp.where(sent, slot, -1)
    chosen = jnp.where(slot == iota((256, COLS), 0), 1.0, 0.0).astype(BF16)
    row = iota((8, COLS), 0)
    tail = jnp.where(row == 0, mu_ref[...], jnp.where(row == 1, albedo_ref[...], 0.0))
    table = jnp.concatenate([t_ref[...] * q_ref[...], tail], axis=0)
    packed = joined(
        lax.dot_general(
            split(table), chosen, (((1,), (1,)), ((), ())), preferred_element_type=F32
        )
    )
    for r, out in enumerate(outs):
        part = packed[:, 64 * r : 64 * r + 64]
        out[...] = jnp.concatenate([part[:40], part[40:]], axis=1)


def regroup_kernel(*refs):
    group = (iota((40, LANES), 1) >> 4) & 3
    for q in range(4):
        out = jnp.zeros((40, LANES), F32)
        for r in range(4):
            moved = refs[r][...]
            if r != q:
                moved = pltpu.roll(moved, (16 * (r - q)) % LANES, 1)
            out = jnp.where(group == r, moved, out)
        refs[4 + q][...] = out


def heat_columns(a_ref, heat_ref, ext_ref, weight_ref, surface_ref, mu, albedo, tiles):
    columns = a_ref.shape[1]
    slope = -1.0 / (DIFFUSIVITY * mu)
    total = jnp.dot(
        ext_ref[:, :LEVELS],
        a_ref[:LEVELS, :],
        precision=lax.Precision.HIGHEST,
        preferred_element_type=F32,
    )
    weight_ref[...] = jnp.broadcast_to(ext_ref[:, LEVELS : LEVELS + 1] * (1.0 / SCALE), (56, LANES))
    for tile in range(columns // LANES):
        at = slice(LANES * tile, LANES * tile + LANES)
        surface_ref[:, at] = (
            weight_ref[...] * albedo[:, at] * jnp.exp2(total[:, at] * (slope[:, at] - 1.0))
        )
    for first in range(0, columns // LANES, tiles):
        spans = [slice(LANES * t, LANES * t + LANES) for t in range(first, first + tiles)]
        slopes = [jnp.broadcast_to(slope[:, at], (8, LANES)) for at in spans]
        start = []
        for at in spans:
            flux = jnp.zeros((8, LANES), F32)
            for o in range(GROUPS):
                flux = flux + (weight_ref[8 * o : 8 * o + 8] - surface_ref[8 * o : 8 * o + 8, at])
            start.append(flux)

        def step(octet, carried, spans=spans, slopes=slopes):
            exts, depths, fluxes = carried
            depths, fluxes = [list(d) for d in depths], list(fluxes)
            base = pl.ds(pl.multiple_of(octet * 8, 8), 8)
            arrays = [a_ref[base, at] for at in spans]
            heats = [[] for _ in spans]
            for s in range(8):
                rows = [jnp.broadcast_to(a[s : s + 1], (8, LANES)) for a in arrays]
                now = [None] * tiles
                for o in range(GROUPS):
                    ext = jnp.broadcast_to(exts[o][:, s : s + 1], (8, LANES))
                    weight = weight_ref[8 * o : 8 * o + 8]
                    for t in range(tiles):
                        depth = depths[o][t] + ext * rows[t]
                        depths[o][t] = depth
                        flux = weight * jnp.exp2(depth * slopes[t]) - surface_ref[
                            8 * o : 8 * o + 8, spans[t]
                        ] * jnp.exp2(depth)
                        now[t] = flux if now[t] is None else now[t] + flux
                for t in range(tiles):
                    heats[t].append(jnp.sum(fluxes[t] - now[t], axis=0, keepdims=True))
                    fluxes[t] = now[t]
            for t in range(tiles):
                heat_ref[base, spans[t]] = jnp.concatenate(heats[t], axis=0)
            exts = [pltpu.roll(e, LANES - 8, 1) for e in exts]
            return exts, depths, fluxes

        zero = jnp.zeros((8, LANES), F32)
        lax.fori_loop(
            0,
            LEVELS // 8,
            step,
            (
                [ext_ref[8 * o : 8 * o + 8] for o in range(GROUPS)],
                [[zero] * tiles for _ in range(GROUPS)],
                start,
            ),
        )


def load_extinction(blocks, ext_ref):
    for k, block in enumerate(blocks):
        ext_ref[14 * k : 14 * k + 14] = block[:14] * SCALE


def octet(count):
    return pl.ds(pl.multiple_of(count * 8, 8), 8)


def spread_row(block, s):
    return jnp.broadcast_to(block[s : s + 1], block.shape)


def sweep(arrays, step, carried, backward=False):
    reads, writes = arrays
    sublane = iota((8, COLS), 0)

    def body(count, carried):
        at = octet(LEVELS // 8 - 1 - count if backward else count)
        blocks = [read(at) for read in reads]
        kept = [None] * len(writes)
        for s in reversed(range(8)) if backward else range(8):
            carried, results = step(carried, *[spread_row(b, s) for b in blocks])
            kept = [r if k is None else jnp.where(sublane == s, r, k) for k, r in zip(kept, results)]
        for write, k in zip(writes, kept):
            write(at, k)
        return carried

    lax.fori_loop(0, LEVELS // 8, body, carried)


def reader(ref, *first):
    return lambda at: ref[(*first, at, slice(None))]


def writer(ref, *first):
    def write(at, value):
        ref[(*first, at, slice(None))] = value

    return write


def factor_kernel(
    q_ref, wind_ref, strength_ref, adjacent_ref,
    inv_ref, down_ref, ratio_ref, tend_ref, avg_ref, correct_ref,
    upper_ref, lower_ref, value_ref,
):
    u, v = wind_ref[0], wind_ref[1]
    mix = strength_ref[...] * (1.0 + ((u[:-1] - u[1:]) ** 2 + (v[:-1] - v[1:]) ** 2))
    edge = jnp.zeros((1, COLS), F32)
    upper_ref[...] = jnp.concatenate([edge, mix], axis=0)
    lower_ref[...] = jnp.concatenate([mix, edge], axis=0)

    def forward(carried, upper, lower, *sides):
        ratio, values = carried
        inverse = 1.0 / ((1.0 + upper + lower) - upper * ratio)
        ratio = lower * inverse
        down = upper * inverse
        values = [side * inverse + down * value for side, value in zip(sides, values)]
        return (ratio, values), (inverse, down, ratio, *values)

    zero = jnp.zeros((8, COLS), F32)
    sides = [reader(q_ref), reader(wind_ref, 0), reader(wind_ref, 1)]
    sweep(
        (
            [reader(upper_ref), reader(lower_ref), *sides],
            [writer(inv_ref), writer(down_ref), writer(ratio_ref)]
            + [writer(value_ref, f) for f in range(3)],
        ),
        forward,
        (zero, [zero] * 3),
    )

    def backward(solved, ratio, *values):
        solved = [value + ratio * x for value, x in zip(values, solved)]
        return solved, solved

    sweep(
        (
            [reader(ratio_ref)] + [reader(value_ref, f) for f in range(3)],
            [writer(value_ref, f) for f in range(3)],
        ),
        backward,
        [zero] * 3,
        True,
    )
    tend_ref[0] = value_ref[0] - q_ref[...]
    tend_ref[1:3] = value_ref[1:3] - wind_ref[...]
    avg = jnp.zeros((LEVELS, LANES), F32)
    for f in range(3):
        avg = avg + times(tend_ref[f], element_mean(f + 1))
    avg_ref[...] = avg
    first = lax.axis_index("elem") * 32
    local = (adjacent_ref[...] - first + 32) & 2047
    spread = jnp.where(iota((32, COLS), 0) == (iota((32, COLS), 1) >> 4), 1.0, 0.0).astype(BF16)
    local = jnp.dot(
        local.astype(F32).astype(BF16), spread, preferred_element_type=F32
    ).astype(jnp.int32)
    row = iota((LANES, COLS), 0)
    weight = jnp.where(row == 32 + (iota((LANES, COLS), 1) >> 4), -2.0, 0.0)
    for k in range(4):
        weight = weight + jnp.where(row == local[k : k + 1], 0.5, 0.0)
    correct_ref[...] = weight.astype(BF16)


def home_kernel(
    e0, e1, e2, e3, t_ref, q_ref, mu_ref, albedo_ref, lit_ref, inv_ref, down_ref, ratio_ref, early_ref,
    tend_ref, avg_ref,
    a_ref, heat_ref, ext_ref, weight_ref, surface_ref,
):
    load_extinction((e0, e1, e2, e3), ext_ref)
    a_ref[...] = t_ref[...] * q_ref[...]
    heat_columns(
        a_ref, heat_ref, ext_ref, weight_ref, surface_ref, mu_ref[...], albedo_ref[...], 2
    )
    side = t_ref[...] + heat_ref[...] * lit_ref[...].astype(F32)
    heat_ref[...] = side * inv_ref[...]


    def forward(value, side, down):
        value = side + down * value
        return value, (value,)

    def backward(solved, value, ratio):
        solved = value + ratio * solved
        return solved, (solved,)

    zero = jnp.zeros((8, COLS), F32)
    writes = [writer(heat_ref)]
    sweep(([reader(heat_ref), reader(down_ref)], writes), forward, zero)
    sweep(([reader(heat_ref), reader(ratio_ref)], writes), backward, zero, True)
    tend = heat_ref[...] - t_ref[...]
    tend_ref[...] = tend
    avg_ref[...] = early_ref[...] + times(tend, element_mean(0))


def span_kernel(
    e0, e1, e2, e3, m0, m1, m2, m3,
    out_ref,
    a_ref, heat_ref, ext_ref, weight_ref, surface_ref,
):
    load_extinction((e0, e1, e2, e3), ext_ref)
    low_half = iota((40, LANES), 1) < 64
    for tile, (a, b) in enumerate(((m0, m1), (m2, m3))):
        a, b = a[...], b[...]
        at = slice(LANES * tile, LANES * tile + LANES)
        a_ref[0:40, at] = jnp.where(low_half, a, pltpu.roll(b, 64, 1))
        a_ref[40:80, at] = jnp.where(low_half, pltpu.roll(a, 64, 1), b)
    mu = a_ref[LEVELS : LEVELS + 1, :]
    albedo = a_ref[LEVELS + 1 : LEVELS + 2, :]
    occupied = mu > 0.0
    heat_columns(
        a_ref, heat_ref, ext_ref, weight_ref, surface_ref, jnp.where(occupied, mu, 1.0), albedo, 2
    )
    place = lax.axis_index("elem") & 15
    heat = jnp.where(occupied, heat_ref[...], 0.0)
    parts = [heat[:, :LANES], heat[:, LANES:]]
    group = iota((LEVELS, LANES), 1) >> 4
    for k in range(3):
        width = 16 << k
        turn = ((place >> k) & 1) == 1
        parts = [
            jnp.where(
                turn,
                jnp.where(
                    ((group >> k) & 1) == 0,
                    pltpu.roll(x, LANES - width, 1),
                    pltpu.roll(x, width, 1),
                ),
                x,
            )
            for x in parts
        ]
    turn = (place >> 3) == 1
    out_ref[:, :LANES] = jnp.where(turn, parts[1], parts[0])
    out_ref[:, LANES:] = jnp.where(turn, parts[0], parts[1])


def finish_kernel(tend0_ref, tend_ref, avg_ref, left_ref, right_ref, correct_ref, out_ref):
    lane = iota((LEVELS, LANES), 1)
    left, own, right = left_ref[...], avg_ref[...], right_ref[...]
    table = correct_ref[...]

    def turned(x, by):
        by = by % LANES
        return pltpu.roll(x, by, 1) if by else x

    for f in range(4):
        wide = jnp.where(
            lane < 32,
            turned(left, -32 * f),
            jnp.where(lane < 64, turned(own, 32 - 32 * f), turned(right, 64 - 32 * f)),
        )
        wide = jnp.where(lane < 96, wide, 0.0)
        tend = tend0_ref[...] if f == 0 else tend_ref[f - 1]
        out_ref[f] = tend + times(wide, table)


def call(kernel, outs, scratch, *args):
    return pl.pallas_call(
        kernel,
        out_shape=outs,
        in_specs=[VMEM] * len(args),
        out_specs=jax.tree.map(lambda _: VMEM, outs),
        scratch_shapes=scratch,
        compiler_params=pltpu.CompilerParams(vmem_limit_bytes=32 * 1024 * 1024),
    )(*args)


def shape(*dims, dtype=F32):
    return jax.ShapeDtypeStruct(dims, dtype)


def number(s, m):
    return 4 * s + m


STAGE_ONE = [
    [(number(s, m), number(s ^ r, m)) for s in range(64) for m in range(4)] for r in range(4)
]
STAGE_TWO = [
    [
        (number(16 * g + i, m), number(16 * m + (i ^ (4 * q)), g))
        for g in range(4)
        for i in range(16)
        for m in range(4)
    ]
    for q in range(4)
]
ROUND = [[(k, (k + step) % 4) for k in range(4)] for step in range(4)]
UP = [(k, (k + 1) % 64) for k in range(64)]
DOWN = [(b, a) for a, b in UP]


def shards(
    thermal_state,
    moisture_content,
    lateral_velocity_components,
    sun_elevation_factor,
    surface_albedo_values,
    turbulent_diffusion_strength,
    sunlit_indicator,
    destination_partition,
    adjacent_elements,
    optical_extinction,
    insolation_quadrature_share,
):
    row = lambda x: x.reshape(1, COLS)
    mu, albedo = row(sun_elevation_factor), row(surface_albedo_values)
    lit, strength = row(sunlit_indicator), row(turbulent_diffusion_strength)
    own_ext = jnp.pad(
        jnp.concatenate([optical_extinction, insolation_quadrature_share[:, None]], axis=1),
        ((0, 2), (0, LANES - LEVELS - 1)),
    )
    exts = [own_ext] + [lax.ppermute(own_ext, "gpt", ROUND[k]) for k in (1, 2, 3)]
    field = shape(LEVELS, COLS)
    block = shape(40, LANES)
    packed = call(
        pack_kernel,
        [block] * 4,
        [],
        thermal_state,
        moisture_content,
        mu,
        albedo,
        lit,
        row(destination_partition),
    )
    gathered = [packed[0]] + [lax.ppermute(packed[r], AXES, STAGE_ONE[r]) for r in (1, 2, 3)]
    inverse, down, ratio, tend_late, early, correct = call(
        factor_kernel,
        [
            field, field, field, shape(3, LEVELS, COLS), shape(LEVELS, LANES),
            shape(LANES, COLS, dtype=BF16),
        ],
        [pltpu.VMEM((LEVELS, COLS), F32)] * 2 + [pltpu.VMEM((3, LEVELS, COLS), F32)],
        moisture_content,
        lateral_velocity_components,
        strength,
        adjacent_elements.T,
    )
    regrouped = call(regroup_kernel, [block] * 4, [], *gathered)
    arrived = [lax.ppermute(regrouped[q], AXES, STAGE_TWO[q]) for q in range(4)]

    def work(columns, rows):
        return [
            pltpu.VMEM((rows, columns), F32),
            pltpu.VMEM((LEVELS, columns), F32),
            pltpu.VMEM((56, LANES), F32),
            pltpu.VMEM((56, LANES), F32),
            pltpu.VMEM((56, columns), F32),
        ]

    tend0, average = call(
        home_kernel,
        [field, shape(LEVELS, LANES)],
        work(COLS, LEVELS),
        *exts, thermal_state, moisture_content, mu, albedo, lit, inverse, down, ratio, early,
    )
    left = lax.ppermute(average, "elem", UP)
    right = lax.ppermute(average, "elem", DOWN)
    span_heating = call(span_kernel, shape(LEVELS, 256), work(256, 80), *exts, *arrived)
    tendency_out = call(
        finish_kernel, shape(4, LEVELS, COLS), [], tend0, tend_late, average, left, right, correct
    )
    return tendency_out, span_heating


def solution(mesh):
    return jax.shard_map(
        shards,
        mesh=mesh,
        in_specs=(
            P(None, "elem"),
            P(None, "elem"),
            P(None, None, "elem"),
            P("elem"),
            P("elem"),
            P("elem"),
            P("elem"),
            P("elem", None),
            P("elem", None),
            P("gpt", None),
            P("gpt"),
        ),
        out_specs=(P(None, None, "elem"), P(None, ("elem", "gpt"))),
        check_vma=False,
    )
```

profile of v0, /device:TPU:4, one launch (start us, length us, event | category | flops | bytes accessed | tf_op | source)
XLA Modules:
  0.0 58.2 jit_solution(12162123251459097384)
XLA Ops:
  0.7 0.7 %copy-done.7 = s32[512]{0:T(512)S(1)} copy-done((s32[512]{0:T(512)S(1)}, s32[512]{0:T(512)}, u32[]{:S(2)}) %copy-start.7) | copy-done | bytes 2072
  1.3 0.0 copy-done.6
  1.3 0.0 copy-done.5
  1.3 0.9 %copy-done = f32[72,512]{1,0:T(8,128)S(1)} copy-done((f32[72,512]{1,0:T(8,128)S(1)}, f32[72,512]{1,0:T(8,128)}, u32[]{:S(2)}) %copy-start) | copy-done | bytes 147480
  2.3 0.9 %copy-done.2 = f32[72,512]{1,0:T(8,128)S(1)} copy-done((f32[72,512]{1,0:T(8,128)S(1)}, f32[72,512]{1,0:T(8,128)}, u32[]{:S(2)}) %copy-start.2) | copy-done | bytes 147480
  3.2 0.7 %copy-done.8 = s32[512,1]{0,1:T(1,128)S(1)} copy-done((s32[512,1]{0,1:T(1,128)S(1)}, s32[512,1]{0,1:T(1,128)}, u32[]{:S(2)}) %copy-start.8) | copy-done | bytes 2072
  3.9 0.6 shard_map.125
  4.4 0.0 copy-start.11
  4.5 0.1 collective-permute-start.5
  4.6 1.7 %collective-permute-start.6 = (f32[40,128]{1,0:T(8,128)S(1)}, f32[40,128]{1,0:T(8,128)S(1)}, u32[]{:S(2)}, u32[]{:S(2)}) collective-permute-start(f32[40,128]{1,0:T(8,128)S(1)} %get-tuple-element.28), channel_id=1, source_target_pairs={{0,8},{1,9},{2,10},{3,11},{4,12},{5,13},{6,14},{7,15},{8,0},{9,1},... | collective-permute-start | bytes 61448 | tf_op jit(solution)/shard_map/ppermute | solution.py:421
  6.2 0.2 collective-permute-start.7
  6.4 0.1 copy.13
  6.5 0.1 select_maximum_fusion.e0
  6.6 1.2 %collective-permute-start = (f32[16,128]{1,0:T(8,128)S(1)}, f32[16,128]{1,0:T(8,128)S(1)}, u32[]{:S(2)}, u32[]{:S(2)}) collective-permute-start(f32[16,128]{1,0:T(8,128)S(1)} %select_maximum_fusion.e0), channel_id=1, source_target_pairs={{0,1},{1,2},{2,3},{3,0},{4,5},{5,6},{6,7},{7,4},{8,9},{9,10},{10,1... | collective-permute-start | bytes 24584 | tf_op jit(solution)/shard_map/ppermute | solution.py:407
  7.8 1.1 %collective-permute-start.1 = (f32[16,128]{1,0:T(8,128)S(1)}, f32[16,128]{1,0:T(8,128)S(1)}, u32[]{:S(2)}, u32[]{:S(2)}) collective-permute-start(f32[16,128]{1,0:T(8,128)S(1)} %select_maximum_fusion.e0), channel_id=1, source_target_pairs={{0,2},{1,3},{2,0},{3,1},{4,6},{5,7},{6,4},{7,5},{8,10},{9,11},{10,... | collective-permute-start | bytes 24584 | tf_op jit(solution)/shard_map/ppermute | solution.py:407
  9.0 2.5 %collective-permute-start.2 = (f32[16,128]{1,0:T(8,128)S(1)}, f32[16,128]{1,0:T(8,128)S(1)}, u32[]{:S(2)}, u32[]{:S(2)}) collective-permute-start(f32[16,128]{1,0:T(8,128)S(1)} %select_maximum_fusion.e0), channel_id=1, source_target_pairs={{0,3},{1,0},{2,1},{3,2},{4,7},{5,4},{6,5},{7,6},{8,11},{9,8},{10,9... | collective-permute-start | bytes 24584 | tf_op jit(solution)/shard_map/ppermute | solution.py:407
  11.5 0.1 shard_map.126
  11.6 0.0 copy-start.10
  11.7 0.0 copy-start.9
  11.7 9.8 %collective-permute-start.8 = (f32[40,128]{1,0:T(8,128)S(1)}, f32[40,128]{1,0:T(8,128)S(1)}, u32[]{:S(2)}, u32[]{:S(2)}) collective-permute-start(f32[40,128]{1,0:T(8,128)S(1)} %get-tuple-element.30), channel_id=1, source_target_pairs={{0,0},{1,64},{2,128},{3,192},{4,4},{5,68},{6,132},{7,196},{8,8},{9... | collective-permute-start | bytes 61448 | tf_op jit(solution)/shard_map/ppermute | solution.py:435
  21.5 0.0 copy-start.4
  21.5 1.0 %copy-done.4 = f32[2,72,512]{2,1,0:T(8,128)S(1)} copy-done((f32[2,72,512]{2,1,0:T(8,128)S(1)}, f32[2,72,512]{2,1,0:T(8,128)}, u32[]{:S(2)}) %copy-start.4) | copy-done | bytes 294936
  22.5 2.0 %shard_map.122 = (f32[72,512]{1,0:T(8,128)S(1)}, f32[72,512]{1,0:T(8,128)S(1)}, f32[72,512]{1,0:T(8,128)S(1)}, f32[3,72,512]{2,1,0:T(8,128)S(1)}, f32[72,128]{1,0:T(8,128)S(1)}, /*index=5*/bf16[128,512]{1,0:T(8,128)(2,1)S(1)}) custom-call(f32[72,512]{1,0:T(8,128)S(1)} %copy-done.1, f32[2,72,512]{2,1,0:T(8,128)S(1)} %copy-done.4, f32[1,512]{1,0:T(1,128)S(1)} %bitcast.14, ...), custom_call_target="tpu_custom_call" | custom-call | tf_op jit(solution)/shard_map/pallas_call | solution.py:352
  24.5 5.2 %shard_map.123 = (f32[72,512]{1,0:T(8,128)S(1)}, f32[72,128]{1,0:T(8,128)S(1)}) custom-call(f32[16,128]{1,0:T(8,128)S(1)} %select_maximum_fusion.e0, f32[16,128]{1,0:T(8,128)S(1)} %collective-permute-done.e1, f32[16,128]{1,0:T(8,128)S(1)} %collective-permute-done.1.e2, f32[16,128]{1,0:T(8,128)S(1)} %collective-permute-done.2.e3, f32[72,512]{1,0:T(8,128)S(1)} %copy-done.3, ...), custom_call_target="tpu_custom_call" | custom-call | tf_op jit(solution)/shard_map/pallas_call | solution.py:352
  29.7 0.1 collective-permute-start.3
  29.8 5.1 %collective-permute-start.4 = (f32[72,128]{1,0:T(8,128)S(1)}, f32[72,128]{1,0:T(8,128)S(1)}, u32[]{:S(2)}, u32[]{:S(2)}) collective-permute-start(f32[72,128]{1,0:T(8,128)S(1)} %get-tuple-element.24.avg_ref), channel_id=1, source_target_pairs={{4,0},{8,4},{12,8},{16,12},{20,16},{24,20},{28,24},{32,28},{36,32}... | collective-permute-start | bytes 110600 | tf_op jit(solution)/shard_map/ppermute | solution.py:453
  34.9 7.2 %collective-permute-start.10 = (f32[40,128]{1,0:T(8,128)S(1)}, f32[40,128]{1,0:T(8,128)S(1)}, u32[]{:S(2)}, u32[]{:S(2)}) collective-permute-start(f32[40,128]{1,0:T(8,128)S(1)} %get-tuple-element.32), channel_id=1, source_target_pairs={{0,32},{1,96},{2,160},{3,224},{4,36},{5,100},{6,164},{7,228},{8,40... | collective-permute-start | bytes 61448 | tf_op jit(solution)/shard_map/ppermute | solution.py:435
  42.1 3.1 %collective-permute-start.11 = (f32[40,128]{1,0:T(8,128)S(1)}, f32[40,128]{1,0:T(8,128)S(1)}, u32[]{:S(2)}, u32[]{:S(2)}) collective-permute-start(f32[40,128]{1,0:T(8,128)S(1)} %get-tuple-element.33), channel_id=1, source_target_pairs={{0,48},{1,112},{2,176},{3,240},{4,52},{5,116},{6,180},{7,244},{8,5... | collective-permute-start | bytes 61448 | tf_op jit(solution)/shard_map/ppermute | solution.py:435
  45.1 2.2 %collective-permute-done.9.m1 = f32[40,128]{1,0:T(8,128)S(1)} collective-permute-done((f32[40,128]{1,0:T(8,128)S(1)}, f32[40,128]{1,0:T(8,128)S(1)}, u32[]{:S(2)}, u32[]{:S(2)}) %collective-permute-start.9) | collective-permute-done | bytes 20512 | tf_op jit(solution)/shard_map/ppermute | solution.py:435
  47.4 6.3 %collective-permute-done.11.m3 = f32[40,128]{1,0:T(8,128)S(1)} collective-permute-done((f32[40,128]{1,0:T(8,128)S(1)}, f32[40,128]{1,0:T(8,128)S(1)}, u32[]{:S(2)}, u32[]{:S(2)}) %collective-permute-start.11) | collective-permute-done | bytes 20512 | tf_op jit(solution)/shard_map/ppermute | solution.py:435
  53.7 3.2 %shard_map.127 = f32[72,256]{1,0:T(8,128)} custom-call(f32[16,128]{1,0:T(8,128)S(1)} %select_maximum_fusion.e0, f32[16,128]{1,0:T(8,128)S(1)} %collective-permute-done.e1, f32[16,128]{1,0:T(8,128)S(1)} %collective-permute-done.1.e2, f32[16,128]{1,0:T(8,128)S(1)} %collective-permute-done.2.e3, f32[40,128]{1,0:T(8,128)S(1)} %collective-permute-done.8.m0, ...), custom_call_target="tpu_custom_call" | custom-call | tf_op jit(solution)/shard_map/pallas_call | solution.py:352
  56.9 1.3 %shard_map.124 = f32[4,72,512]{2,1,0:T(8,128)} custom-call(f32[72,512]{1,0:T(8,128)S(1)} %get-tuple-element.22.tend0_ref, f32[3,72,512]{2,1,0:T(8,128)S(1)} %get-tuple-element.23.tend_ref, f32[72,128]{1,0:T(8,128)S(1)} %get-tuple-element.24.avg_ref, f32[72,128]{1,0:T(8,128)S(1)} %collective-permute-done.3.left_ref, ...), custom_call_target="tpu_custom_call" | custom-call | tf_op jit(solution)/shard_map/pallas_call | solution.py:352
  (26 shorter events, 0.1 us)
Async XLA Ops:
  0.6 0.7 %copy-start.7 = (s32[512]{0:T(512)S(1)}, s32[512]{0:T(512)}, u32[]{:S(2)}) copy-start(s32[512]{0:T(512)} %param.17) | copy-start | bytes 6148
  0.6 0.7 %copy-start.6 = (f32[512]{0:T(512)S(1)}, f32[512]{0:T(512)}, u32[]{:S(2)}) copy-start(f32[512]{0:T(512)} %param.15) | copy-start | bytes 6148
  0.7 0.7 %copy-start.5 = (f32[512]{0:T(512)S(1)}, f32[512]{0:T(512)}, u32[]{:S(2)}) copy-start(f32[512]{0:T(512)} %param.14) | copy-start | bytes 6148
  1.3 0.9 %copy-start = (f32[72,512]{1,0:T(8,128)S(1)}, f32[72,512]{1,0:T(8,128)}, u32[]{:S(2)}) copy-start(f32[72,512]{1,0:T(8,128)} %q_ref.5) | copy-start | bytes 442372
  2.3 0.9 %copy-start.2 = (f32[72,512]{1,0:T(8,128)S(1)}, f32[72,512]{1,0:T(8,128)}, u32[]{:S(2)}) copy-start(f32[72,512]{1,0:T(8,128)} %t_ref.3) | copy-start | bytes 442372
  3.2 0.7 %copy-start.8 = (s32[512,1]{0,1:T(1,128)S(1)}, s32[512,1]{0,1:T(1,128)}, u32[]{:S(2)}) copy-start(s32[512,1]{0,1:T(1,128)} %param.18) | copy-start | bytes 6148
  3.8 2.6 %copy-start.12 = (f32[14]{0:T(128)S(1)}, f32[14]{0:T(128)}, u32[]{:S(2)}) copy-start(f32[14]{0:T(128)} %param.21) | copy-start | bytes 172
  3.9 17.6 %copy-start.1 = (f32[72,512]{1,0:T(8,128)S(1)}, f32[72,512]{1,0:T(8,128)}, u32[]{:S(2)}) copy-start(f32[72,512]{1,0:T(8,128)} %q_ref.5) | copy-start | bytes 442372
  4.4 2.1 %copy-start.11 = (f32[14,72]{1,0:T(8,128)S(1)}, f32[14,72]{1,0:T(8,128)}, u32[]{:S(2)}) copy-start(f32[14,72]{1,0:T(8,128)} %param.20) | copy-start | bytes 12100
  4.5 4.5 %collective-permute-start.5 = (f32[40,128]{1,0:T(8,128)S(1)}, f32[40,128]{1,0:T(8,128)S(1)}, u32[]{:S(2)}, u32[]{:S(2)}) collective-permute-start(f32[40,128]{1,0:T(8,128)S(1)} %get-tuple-element.27), channel_id=1, source_target_pairs={{0,4},{1,5},{2,6},{3,7},{4,0},{5,1},{6,2},{7,3},{8,12},{9,13},{10,... | collective-permute-start | bytes 61448 | tf_op jit(solution)/shard_map/ppermute | solution.py:421
  4.6 7.0 %collective-permute-start.6 = (f32[40,128]{1,0:T(8,128)S(1)}, f32[40,128]{1,0:T(8,128)S(1)}, u32[]{:S(2)}, u32[]{:S(2)}) collective-permute-start(f32[40,128]{1,0:T(8,128)S(1)} %get-tuple-element.28), channel_id=1, source_target_pairs={{0,8},{1,9},{2,10},{3,11},{4,12},{5,13},{6,14},{7,15},{8,0},{9,1},... | collective-permute-start | bytes 61448 | tf_op jit(solution)/shard_map/ppermute | solution.py:421
  6.2 5.3 %collective-permute-start.7 = (f32[40,128]{1,0:T(8,128)S(1)}, f32[40,128]{1,0:T(8,128)S(1)}, u32[]{:S(2)}, u32[]{:S(2)}) collective-permute-start(f32[40,128]{1,0:T(8,128)S(1)} %get-tuple-element.29), channel_id=1, source_target_pairs={{0,12},{1,13},{2,14},{3,15},{4,8},{5,9},{6,10},{7,11},{8,4},{9,5},... | collective-permute-start | bytes 61448 | tf_op jit(solution)/shard_map/ppermute | solution.py:421
  6.6 17.9 %collective-permute-start = (f32[16,128]{1,0:T(8,128)S(1)}, f32[16,128]{1,0:T(8,128)S(1)}, u32[]{:S(2)}, u32[]{:S(2)}) collective-permute-start(f32[16,128]{1,0:T(8,128)S(1)} %select_maximum_fusion.e0), channel_id=1, source_target_pairs={{0,1},{1,2},{2,3},{3,0},{4,5},{5,6},{6,7},{7,4},{8,9},{9,10},{10,1... | collective-permute-start | bytes 24584 | tf_op jit(solution)/shard_map/ppermute | solution.py:407
  7.8 16.7 %collective-permute-start.1 = (f32[16,128]{1,0:T(8,128)S(1)}, f32[16,128]{1,0:T(8,128)S(1)}, u32[]{:S(2)}, u32[]{:S(2)}) collective-permute-start(f32[16,128]{1,0:T(8,128)S(1)} %select_maximum_fusion.e0), channel_id=1, source_target_pairs={{0,2},{1,3},{2,0},{3,1},{4,6},{5,7},{6,4},{7,5},{8,10},{9,11},{10,... | collective-permute-start | bytes 24584 | tf_op jit(solution)/shard_map/ppermute | solution.py:407
  9.0 15.6 %collective-permute-start.2 = (f32[16,128]{1,0:T(8,128)S(1)}, f32[16,128]{1,0:T(8,128)S(1)}, u32[]{:S(2)}, u32[]{:S(2)}) collective-permute-start(f32[16,128]{1,0:T(8,128)S(1)} %select_maximum_fusion.e0), channel_id=1, source_target_pairs={{0,3},{1,0},{2,1},{3,2},{4,7},{5,4},{6,5},{7,6},{8,11},{9,8},{10,9... | collective-permute-start | bytes 24584 | tf_op jit(solution)/shard_map/ppermute | solution.py:407
  11.6 9.9 %copy-start.10 = (s32[32,4]{0,1:T(4,128)S(1)}, s32[32,4]{0,1:T(4,128)}, u32[]{:S(2)}) copy-start(s32[32,4]{0,1:T(4,128)} %param.19) | copy-start | bytes 1540
  11.7 9.9 %copy-start.9 = (f32[512]{0:T(512)S(1)}, f32[512]{0:T(512)}, u32[]{:S(2)}) copy-start(f32[512]{0:T(512)} %param.16) | copy-start | bytes 6148
  11.7 30.4 %collective-permute-start.8 = (f32[40,128]{1,0:T(8,128)S(1)}, f32[40,128]{1,0:T(8,128)S(1)}, u32[]{:S(2)}, u32[]{:S(2)}) collective-permute-start(f32[40,128]{1,0:T(8,128)S(1)} %get-tuple-element.30), channel_id=1, source_target_pairs={{0,0},{1,64},{2,128},{3,192},{4,4},{5,68},{6,132},{7,196},{8,8},{9... | collective-permute-start | bytes 61448 | tf_op jit(solution)/shard_map/ppermute | solution.py:435
  21.5 1.0 %copy-start.4 = (f32[2,72,512]{2,1,0:T(8,128)S(1)}, f32[2,72,512]{2,1,0:T(8,128)}, u32[]{:S(2)}) copy-start(f32[2,72,512]{2,1,0:T(8,128)} %wind_ref.1) | copy-start | bytes 884740
  22.5 2.0 %copy-start.3 = (f32[72,512]{1,0:T(8,128)S(1)}, f32[72,512]{1,0:T(8,128)}, u32[]{:S(2)}) copy-start(f32[72,512]{1,0:T(8,128)} %t_ref.3) | copy-start | bytes 442372
  29.7 27.2 %collective-permute-start.3 = (f32[72,128]{1,0:T(8,128)S(1)}, f32[72,128]{1,0:T(8,128)S(1)}, u32[]{:S(2)}, u32[]{:S(2)}) collective-permute-start(f32[72,128]{1,0:T(8,128)S(1)} %get-tuple-element.24.avg_ref), channel_id=1, source_target_pairs={{0,4},{4,8},{8,12},{12,16},{16,20},{20,24},{24,28},{28,32},{32,36}... | collective-permute-start | bytes 110600 | tf_op jit(solution)/shard_map/ppermute | solution.py:452
  29.8 27.1 %collective-permute-start.4 = (f32[72,128]{1,0:T(8,128)S(1)}, f32[72,128]{1,0:T(8,128)S(1)}, u32[]{:S(2)}, u32[]{:S(2)}) collective-permute-start(f32[72,128]{1,0:T(8,128)S(1)} %get-tuple-element.24.avg_ref), channel_id=1, source_target_pairs={{4,0},{8,4},{12,8},{16,12},{20,16},{24,20},{28,24},{32,28},{36,32}... | collective-permute-start | bytes 110600 | tf_op jit(solution)/shard_map/ppermute | solution.py:453
  34.9 12.5 %collective-permute-start.9 = (f32[40,128]{1,0:T(8,128)S(1)}, f32[40,128]{1,0:T(8,128)S(1)}, u32[]{:S(2)}, u32[]{:S(2)}) collective-permute-start(f32[40,128]{1,0:T(8,128)S(1)} %get-tuple-element.31), channel_id=1, source_target_pairs={{0,16},{1,80},{2,144},{3,208},{4,20},{5,84},{6,148},{7,212},{8,24}... | collective-permute-start | bytes 61448 | tf_op jit(solution)/shard_map/ppermute | solution.py:435
  34.9 12.5 %collective-permute-start.10 = (f32[40,128]{1,0:T(8,128)S(1)}, f32[40,128]{1,0:T(8,128)S(1)}, u32[]{:S(2)}, u32[]{:S(2)}) collective-permute-start(f32[40,128]{1,0:T(8,128)S(1)} %get-tuple-element.32), channel_id=1, source_target_pairs={{0,32},{1,96},{2,160},{3,224},{4,36},{5,100},{6,164},{7,228},{8,40... | collective-permute-start | bytes 61448 | tf_op jit(solution)/shard_map/ppermute | solution.py:435
  42.1 11.6 %collective-permute-start.11 = (f32[40,128]{1,0:T(8,128)S(1)}, f32[40,128]{1,0:T(8,128)S(1)}, u32[]{:S(2)}, u32[]{:S(2)}) collective-permute-start(f32[40,128]{1,0:T(8,128)S(1)} %get-tuple-element.33), channel_id=1, source_target_pairs={{0,48},{1,112},{2,176},{3,240},{4,52},{5,116},{6,180},{7,244},{8,5... | collective-permute-start | bytes 61448 | tf_op jit(solution)/shard_map/ppermute | solution.py:435
where the time goes:
time: 58.4 us; the launch traced here: 58.2 us
  starting transfers between devices  32.1 us (55%)
  Pallas kernels  12.4 us (21%)
  waiting for transfers between devices  8.53 us (15%)
  local copies, waits for them, and re-layouts  4.27 us (7%)
  between operations  0.81 us (1%)
    ppermute x4, starting transfers between devices, shards(): arrived = [lax.ppermute(regrouped[q], AXES, STAGE_TWO[q]) for q in range(4)]  20.1 us
    pallas_call x6, Pallas kernels, call(): pl.pallas_call(kernel, out_shape=outs, in_specs=[VMEM] * len(args), out_s...  12.4 us
    ppermute x4, waiting for transfers between devices, shards(): arrived = [lax.ppermute(regrouped[q], AXES, STAGE_TWO[q]) for q in range(4)]  8.51 us
    ppermute x1, starting transfers between devices, shards(): right = lax.ppermute(average, 'elem', DOWN)  5.05 us
    ppermute x3, starting transfers between devices, shards(): lax.ppermute(own_ext, 'gpt', ROUND[k])  4.9 us
    unnamed x26, local copies, waits for them, and re-layouts  4.18 us
    ppermute x3, starting transfers between devices, shards(): lax.ppermute(packed[r], AXES, STAGE_ONE[r])  1.96 us
  transfers between devices with their start and end apart: 12, of which 2 were waited for; matrix products, arithmetic and copies ran while one was open for 0% of the time, Pallas kernels for 18%

commit v1 on v0

--- a/solution.py
+++ b/solution.py
@@ -12,6 +12,7 @@
 COLS = 512
 EPTS = 16
 LANES = 128
+WIDE = 1280
 GROUPS = 7
 DIFFUSIVITY = 1.66
 SCALE = DIFFUSIVITY * math.log2(math.e)
@@ -47,18 +48,44 @@
     return jnp.where(iota((COLS, LANES), 1) == at, 1.0 / EPTS, 0.0).astype(BF16)
 
 
-def pack_kernel(t_ref, q_ref, mu_ref, albedo_ref, lit_ref, dest_ref, *outs):
-    place = lax.axis_index("elem") & 15
-    member = lax.axis_index("gpt")
+def swap_groups(x):
+    sublane, group = iota((8, LANES), 0), iota((8, LANES), 1) >> 4
+    for k in range(3):
+        height, width = 1 << k, 16 << k
+        up = pltpu.roll(pltpu.roll(x, 8 - height, 0), width, 1)
+        down = pltpu.roll(pltpu.roll(x, height, 0), LANES - width, 1)
+        in_row, in_lane = (sublane >> k) & 1, (group >> k) & 1
+        x = jnp.where(in_row == in_lane, x, jnp.where(in_row == 0, up, down))
+    return x
+
+
+STRENGTH, LIT, ADJACENT, MU, ALBEDO = 0, 1, 2, 6, 7
+
+
+def pack_kernel(
+    t_ref, q_ref, mu_ref, albedo_ref, lit_ref, dest_ref, strength_ref, adjacent_ref,
+    low_ref, high_ref, scalar_ref,
+):
+    scalar_ref[STRENGTH : STRENGTH + 1] = strength_ref[...]
+    scalar_ref[LIT : LIT + 1] = lit_ref[...].astype(F32)
+    scalar_ref[ADJACENT:MU, :32] = adjacent_ref[...].astype(F32)
+    scalar_ref[MU : MU + 1] = mu_ref[...]
+    scalar_ref[ALBEDO : ALBEDO + 1] = albedo_ref[...]
+    served = (2 * (lax.axis_index("elem") >> 4) + 2 - lax.axis_index("gpt")) & 3
+    before = jnp.where(iota((LANES, LANES), 0) < iota((LANES, LANES), 1), 1.0, 0.0).astype(BF16)
     dest = dest_ref[...]
-    onehot = jnp.where(dest == iota((64, COLS), 0), 1.0, 0.0)
-    before = jnp.where(iota((COLS, COLS), 0) < iota((COLS, COLS), 1), 1.0, 0.0).astype(BF16)
-    earlier = jnp.dot(onehot.astype(BF16), before, preferred_element_type=F32)
-    rank = jnp.sum(onehot * earlier, axis=0, keepdims=True).astype(jnp.int32)
-    apart = (dest & 15) ^ place
-    slot = (apart & 3) * 64 + (apart >> 2) * 16 + rank
-    sent = ((dest >> 4) == member) & (lit_ref[...] != 0)
-    slot = jnp.where(sent, slot, -1)
+    number_of = iota((64, LANES), 0)
+    gone = jnp.zeros((64, 1), F32)
+    ranks = []
+    for tile in range(COLS // LANES):
+        onehot = jnp.where(dest[:, LANES * tile : LANES * tile + LANES] == number_of, 1.0, 0.0)
+        earlier = jnp.dot(onehot.astype(BF16), before, preferred_element_type=F32)
+        ranks.append(jnp.sum(onehot * (earlier + gone), axis=0, keepdims=True))
+        gone = gone + jnp.sum(onehot, axis=1, keepdims=True)
+    rank = jnp.concatenate(ranks, axis=1).astype(jnp.int32)
+    sent = ((dest >> 4) == served) & (lit_ref[...] != 0)
+    apart = (dest ^ lax.axis_index("elem")) & 15
+    slot = jnp.where(sent, apart * 16 + rank, -1)
     chosen = jnp.where(slot == iota((256, COLS), 0), 1.0, 0.0).astype(BF16)
     row = iota((8, COLS), 0)
     tail = jnp.where(row == 0, mu_ref[...], jnp.where(row == 1, albedo_ref[...], 0.0))
@@ -68,21 +95,49 @@
             split(table), chosen, (((1,), (1,)), ((), ())), preferred_element_type=F32
         )
     )
-    for r, out in enumerate(outs):
-        part = packed[:, 64 * r : 64 * r + 64]
-        out[...] = jnp.concatenate([part[:40], part[40:]], axis=1)
-
-
-def regroup_kernel(*refs):
-    group = (iota((40, LANES), 1) >> 4) & 3
-    for q in range(4):
-        out = jnp.zeros((40, LANES), F32)
-        for r in range(4):
-            moved = refs[r][...]
-            if r != q:
-                moved = pltpu.roll(moved, (16 * (r - q)) % LANES, 1)
-            out = jnp.where(group == r, moved, out)
-        refs[4 + q][...] = out
+    for half, out_ref in enumerate((low_ref, high_ref)):
+        for o in range(10):
+            part = packed[8 * o : 8 * o + 8, LANES * half : LANES * half + LANES]
+            at = slice(LANES * o, LANES * o + LANES)
+            out_ref[:, at] = swap_groups(part)
+
+
+def bit_of_row(bit):
+    return (iota((8, WIDE), 0) >> bit) & 1
+
+
+def taken(low, high, bit):
+    return jnp.where(bit_of_row(bit) == 0, pltpu.roll(low, 8 - (1 << bit), 0), high)
+
+
+def put(low, high, got, bit):
+    clear = bit_of_row(bit) == 0
+    return jnp.where(clear, low, pltpu.roll(got, 1 << bit, 0)), jnp.where(clear, high, got)
+
+
+def held(blocks):
+    low, high = blocks[0][...], blocks[1][...]
+    for bit, got in zip((2, 1, 0), blocks[2:]):
+        low, high = put(low, high, got[...], bit)
+    return low, high
+
+
+def pair_kernel(own_ref, beside_ref, exts_ref):
+    exts_ref[:16] = own_ref[...]
+    exts_ref[16:] = beside_ref[...]
+
+
+def next_kernel(*refs):
+    *blocks, out_ref = refs
+    low, high = held(blocks)
+    out_ref[...] = taken(low, high, 4 - len(blocks))
+
+
+def last_kernel(b0, b1, b2, b3, avg_ref, out_ref):
+    low, high = held((b0, b1, b2, b3))
+    out_ref[:, :WIDE] = taken(low, high, 0)
+    for o in range(LEVELS // 8):
+        out_ref[:, WIDE + LANES * o : WIDE + LANES * o + LANES] = avg_ref[8 * o : 8 * o + 8]
 
 
 def heat_columns(a_ref, heat_ref, ext_ref, weight_ref, surface_ref, mu, albedo, tiles):
@@ -151,8 +206,9 @@
 
 
 def load_extinction(blocks, ext_ref):
-    for k, block in enumerate(blocks):
-        ext_ref[14 * k : 14 * k + 14] = block[:14] * SCALE
+    for k in range(4):
+        at = 16 * (k & 1)
+        ext_ref[14 * k : 14 * k + 14] = blocks[k >> 1][at : at + 14] * SCALE
 
 
 def octet(count):
@@ -193,12 +249,23 @@
 
 
 def factor_kernel(
-    q_ref, wind_ref, strength_ref, adjacent_ref,
+    scalar_ref, q_ref, wind_ref,
     inv_ref, down_ref, ratio_ref, tend_ref, avg_ref, correct_ref,
     upper_ref, lower_ref, value_ref,
 ):
+    spread = jnp.where(iota((32, COLS), 0) == (iota((32, COLS), 1) >> 4), 1.0, 0.0).astype(BF16)
+    row = iota((LANES, COLS), 0)
+    weight = jnp.where(row == 32 + (iota((LANES, COLS), 1) >> 4), -2.0, 0.0)
+    first = lax.axis_index("elem") * 32
+    local = (scalar_ref[ADJACENT:MU, :32].astype(jnp.int32) - first + 32) & 2047
+    local = jnp.dot(
+        local.astype(F32).astype(BF16), spread, preferred_element_type=F32
+    ).astype(jnp.int32)
+    for k in range(4):
+        weight = weight + jnp.where(row == local[k : k + 1], 0.5, 0.0)
+    correct_ref[...] = weight.astype(BF16)
     u, v = wind_ref[0], wind_ref[1]
-    mix = strength_ref[...] * (1.0 + ((u[:-1] - u[1:]) ** 2 + (v[:-1] - v[1:]) ** 2))
+    mix = scalar_ref[STRENGTH : STRENGTH + 1] * (1.0 + ((u[:-1] - u[1:]) ** 2 + (v[:-1] - v[1:]) ** 2))
     edge = jnp.zeros((1, COLS), F32)
     upper_ref[...] = jnp.concatenate([edge, mix], axis=0)
     lower_ref[...] = jnp.concatenate([mix, edge], axis=0)
@@ -242,32 +309,21 @@
     for f in range(3):
         avg = avg + times(tend_ref[f], element_mean(f + 1))
     avg_ref[...] = avg
-    first = lax.axis_index("elem") * 32
-    local = (adjacent_ref[...] - first + 32) & 2047
-    spread = jnp.where(iota((32, COLS), 0) == (iota((32, COLS), 1) >> 4), 1.0, 0.0).astype(BF16)
-    local = jnp.dot(
-        local.astype(F32).astype(BF16), spread, preferred_element_type=F32
-    ).astype(jnp.int32)
-    row = iota((LANES, COLS), 0)
-    weight = jnp.where(row == 32 + (iota((LANES, COLS), 1) >> 4), -2.0, 0.0)
-    for k in range(4):
-        weight = weight + jnp.where(row == local[k : k + 1], 0.5, 0.0)
-    correct_ref[...] = weight.astype(BF16)
 
 
 def home_kernel(
-    e0, e1, e2, e3, t_ref, q_ref, mu_ref, albedo_ref, lit_ref, inv_ref, down_ref, ratio_ref, early_ref,
-    tend_ref, avg_ref,
-    a_ref, heat_ref, ext_ref, weight_ref, surface_ref,
+    e0, e1, t_ref, q_ref, scalar_ref, out_ref, a_ref, ext_ref, weight_ref, surface_ref
 ):
-    load_extinction((e0, e1, e2, e3), ext_ref)
+    load_extinction((e0, e1), ext_ref)
     a_ref[...] = t_ref[...] * q_ref[...]
-    heat_columns(
-        a_ref, heat_ref, ext_ref, weight_ref, surface_ref, mu_ref[...], albedo_ref[...], 2
-    )
-    side = t_ref[...] + heat_ref[...] * lit_ref[...].astype(F32)
+    mu, albedo = scalar_ref[MU : MU + 1], scalar_ref[ALBEDO : ALBEDO + 1]
+    heat_columns(a_ref, out_ref, ext_ref, weight_ref, surface_ref, mu, albedo, 4)
+    out_ref[...] = out_ref[...] * scalar_ref[LIT : LIT + 1]
+
+
+def solve_kernel(t_ref, flux_ref, inv_ref, down_ref, ratio_ref, early_ref, tend_ref, avg_ref, heat_ref):
+    side = t_ref[...] + flux_ref[...]
     heat_ref[...] = side * inv_ref[...]
-
 
     def forward(value, side, down):
         value = side + down * value
@@ -287,50 +343,48 @@
 
 
 def span_kernel(
-    e0, e1, e2, e3, m0, m1, m2, m3,
-    out_ref,
+    e0, e1, b0, b1, b2, b3, last_ref, out_ref, token_ref,
     a_ref, heat_ref, ext_ref, weight_ref, surface_ref,
 ):
-    load_extinction((e0, e1, e2, e3), ext_ref)
-    low_half = iota((40, LANES), 1) < 64
-    for tile, (a, b) in enumerate(((m0, m1), (m2, m3))):
-        a, b = a[...], b[...]
-        at = slice(LANES * tile, LANES * tile + LANES)
-        a_ref[0:40, at] = jnp.where(low_half, a, pltpu.roll(b, 64, 1))
-        a_ref[40:80, at] = jnp.where(low_half, pltpu.roll(a, 64, 1), b)
+    load_extinction((e0, e1), ext_ref)
+    place = lax.axis_index("elem")
+    halves = list(held((b0, b1, b2, b3, last_ref.at[:, :WIDE])))
+    for bit in range(3):
+        turn = ((place >> bit) & 1) == 1
+        height = 1 << bit
+        clear = bit_of_row(bit) == 0
+        halves = [
+            jnp.where(
+                turn, jnp.where(clear, pltpu.roll(x, 8 - height, 0), pltpu.roll(x, height, 0)), x
+            )
+            for x in halves
+        ]
+    turn = ((place >> 3) & 1) == 1
+    low, high = halves
+    halves = (jnp.where(turn, high, low), jnp.where(turn, low, high))
+    for half in range(2):
+        for o in range(10):
+            a_ref[8 * o : 8 * o + 8, LANES * half : LANES * half + LANES] = swap_groups(
+                halves[half][:, LANES * o : LANES * o + LANES]
+            )
     mu = a_ref[LEVELS : LEVELS + 1, :]
     albedo = a_ref[LEVELS + 1 : LEVELS + 2, :]
     occupied = mu > 0.0
     heat_columns(
         a_ref, heat_ref, ext_ref, weight_ref, surface_ref, jnp.where(occupied, mu, 1.0), albedo, 2
     )
-    place = lax.axis_index("elem") & 15
-    heat = jnp.where(occupied, heat_ref[...], 0.0)
-    parts = [heat[:, :LANES], heat[:, LANES:]]
-    group = iota((LEVELS, LANES), 1) >> 4
-    for k in range(3):
-        width = 16 << k
-        turn = ((place >> k) & 1) == 1
-        parts = [
-            jnp.where(
-                turn,
-                jnp.where(
-                    ((group >> k) & 1) == 0,
-                    pltpu.roll(x, LANES - width, 1),
-                    pltpu.roll(x, width, 1),
-                ),
-                x,
-            )
-            for x in parts
-        ]
-    turn = (place >> 3) == 1
-    out_ref[:, :LANES] = jnp.where(turn, parts[1], parts[0])
-    out_ref[:, LANES:] = jnp.where(turn, parts[0], parts[1])
-
-
-def finish_kernel(tend0_ref, tend_ref, avg_ref, left_ref, right_ref, correct_ref, out_ref):
+    out_ref[...] = jnp.where(occupied, heat_ref[...], 0.0)
+    token_ref[...] = jnp.zeros_like(token_ref)
+
+
+def finish_kernel(tend0_ref, tend_ref, avg_ref, chip_ref, off_ref, correct_ref, out_ref):
     lane = iota((LEVELS, LANES), 1)
-    left, own, right = left_ref[...], avg_ref[...], right_ref[...]
+    first = (lax.axis_index("elem") & 1) == 0
+    own, off = avg_ref[...], off_ref[...]
+    chip = jnp.concatenate(
+        [chip_ref[:, WIDE + LANES * o : WIDE + LANES * o + LANES] for o in range(LEVELS // 8)], axis=0
+    )
+    left, right = jnp.where(first, off, chip), jnp.where(first, chip, off)
     table = correct_ref[...]
 
     def turned(x, by):
@@ -348,15 +402,20 @@
         out_ref[f] = tend + times(wide, table)
 
 
-def call(kernel, outs, scratch, *args):
+def call(kernel, outs, scratch, *args, limit=32, after=()):
+    idle = len(after)
+
+    def body(*refs):
+        kernel(*refs[: len(args)], *refs[len(args) + idle :])
+
     return pl.pallas_call(
-        kernel,
+        body,
         out_shape=outs,
-        in_specs=[VMEM] * len(args),
+        in_specs=[VMEM] * len(args) + [pl.BlockSpec(memory_space=pl.ANY)] * idle,
         out_specs=jax.tree.map(lambda _: VMEM, outs),
         scratch_shapes=scratch,
-        compiler_params=pltpu.CompilerParams(vmem_limit_bytes=32 * 1024 * 1024),
-    )(*args)
+        compiler_params=pltpu.CompilerParams(vmem_limit_bytes=limit * 1024 * 1024),
+    )(*args, *after)
 
 
 def shape(*dims, dtype=F32):
@@ -367,21 +426,26 @@
     return 4 * s + m
 
 
-STAGE_ONE = [
-    [(number(s, m), number(s ^ r, m)) for s in range(64) for m in range(4)] for r in range(4)
+BESIDE = [(number(s, m), number(s, m ^ 1)) for s in range(64) for m in range(4)]
+OPPOSITE = [(number(s, m), number(s, m ^ 2)) for s in range(64) for m in range(4)]
+SWAPS = [
+    [(number(s, m), number(s ^ (1 << bit), m)) for s in range(64) for m in range(4)]
+    for bit in range(4)
 ]
-STAGE_TWO = [
+ACROSS = [
     [
-        (number(16 * g + i, m), number(16 * m + (i ^ (4 * q)), g))
+        (number(16 * g + i, m), number(16 * ((2 * g + 2 - m) % 4) + (i ^ flip), g))
         for g in range(4)
         for i in range(16)
         for m in range(4)
     ]
-    for q in range(4)
+    for flip in (0, 8)
 ]
-ROUND = [[(k, (k + step) % 4) for k in range(4)] for step in range(4)]
-UP = [(k, (k + 1) % 64) for k in range(64)]
-DOWN = [(b, a) for a, b in UP]
+OFF_CHIP = [
+    (number(s, m), number((s - 1 if s % 2 == 0 else s + 1) % 64, m))
+    for s in range(64)
+    for m in range(4)
+]
 
 
 def shards(
@@ -400,16 +464,15 @@
     row = lambda x: x.reshape(1, COLS)
     mu, albedo = row(sun_elevation_factor), row(surface_albedo_values)
     lit, strength = row(sunlit_indicator), row(turbulent_diffusion_strength)
+    field = shape(LEVELS, COLS)
+    message = shape(8, WIDE)
     own_ext = jnp.pad(
         jnp.concatenate([optical_extinction, insolation_quadrature_share[:, None]], axis=1),
         ((0, 2), (0, LANES - LEVELS - 1)),
     )
-    exts = [own_ext] + [lax.ppermute(own_ext, "gpt", ROUND[k]) for k in (1, 2, 3)]
-    field = shape(LEVELS, COLS)
-    block = shape(40, LANES)
-    packed = call(
+    low, high, scalars = call(
         pack_kernel,
-        [block] * 4,
+        [message, message, shape(8, COLS)],
         [],
         thermal_state,
         moisture_content,
@@ -417,43 +480,68 @@
         albedo,
         lit,
         row(destination_partition),
-    )
-    gathered = [packed[0]] + [lax.ppermute(packed[r], AXES, STAGE_ONE[r]) for r in (1, 2, 3)]
+        strength,
+        adjacent_elements.T,
+        limit=60,
+    )
+    blocks = [lax.ppermute(x, AXES, pairs) for x, pairs in zip((low, high), ACROSS)]
+    beside = lax.ppermute(own_ext, AXES, BESIDE)
+    pair = call(pair_kernel, shape(32, LANES), [], own_ext, beside)
+    exts = (pair, lax.ppermute(pair, AXES, OPPOSITE))
     inverse, down, ratio, tend_late, early, correct = call(
         factor_kernel,
         [
             field, field, field, shape(3, LEVELS, COLS), shape(LEVELS, LANES),
             shape(LANES, COLS, dtype=BF16),
         ],
-        [pltpu.VMEM((LEVELS, COLS), F32)] * 2 + [pltpu.VMEM((3, LEVELS, COLS), F32)],
+        [
+            *[pltpu.VMEM((LEVELS, COLS), F32)] * 2,
+            pltpu.VMEM((3, LEVELS, COLS), F32),
+        ],
+        scalars,
         moisture_content,
         lateral_velocity_components,
-        strength,
-        adjacent_elements.T,
-    )
-    regrouped = call(regroup_kernel, [block] * 4, [], *gathered)
-    arrived = [lax.ppermute(regrouped[q], AXES, STAGE_TWO[q]) for q in range(4)]
-
-    def work(columns, rows):
+        after=(pair,),
+    )
+
+    def tables(columns):
         return [
-            pltpu.VMEM((rows, columns), F32),
-            pltpu.VMEM((LEVELS, columns), F32),
             pltpu.VMEM((56, LANES), F32),
             pltpu.VMEM((56, LANES), F32),
             pltpu.VMEM((56, columns), F32),
         ]
 
+    sent = call(next_kernel, message, [], *blocks, after=(early, exts[1]))
+    blocks.append(lax.ppermute(sent, AXES, SWAPS[2]))
+    heat = call(
+        home_kernel,
+        field,
+        [pltpu.VMEM((LEVELS, COLS), F32), *tables(COLS)],
+        *exts, thermal_state, moisture_content, scalars,
+        after=(sent,),
+    )
+    sent = call(next_kernel, message, [], *blocks, after=(heat,))
+    blocks.append(lax.ppermute(sent, AXES, SWAPS[1]))
     tend0, average = call(
-        home_kernel,
+        solve_kernel,
         [field, shape(LEVELS, LANES)],
-        work(COLS, LEVELS),
-        *exts, thermal_state, moisture_content, mu, albedo, lit, inverse, down, ratio, early,
-    )
-    left = lax.ppermute(average, "elem", UP)
-    right = lax.ppermute(average, "elem", DOWN)
-    span_heating = call(span_kernel, shape(LEVELS, 256), work(256, 80), *exts, *arrived)
+        [pltpu.VMEM((LEVELS, COLS), F32)],
+        thermal_state, heat, inverse, down, ratio, early,
+        after=(sent,),
+    )
+    off = lax.ppermute(average, AXES, OFF_CHIP)
+    sent = call(last_kernel, shape(8, WIDE + LEVELS * 16), [], *blocks, average)
+    last = lax.ppermute(sent, AXES, SWAPS[0])
+    span_heating, token = call(
+        span_kernel,
+        [shape(LEVELS, 256), shape(8, LANES)],
+        [pltpu.VMEM((80, 256), F32), pltpu.VMEM((LEVELS, 256), F32), *tables(256)],
+        *exts, *blocks, last,
+    )
     tendency_out = call(
-        finish_kernel, shape(4, LEVELS, COLS), [], tend0, tend_late, average, left, right, correct
+        finish_kernel, shape(4, LEVELS, COLS), [],
+        tend0, tend_late, average, last, off, correct,
+        after=(token,),
     )
     return tendency_out, span_heating
 

time: 58.4 us -> 40.3 us (0.69)
  the two profiles are of different devices: /device:TPU:4 before, /device:TPU:2 now
where the time goes in v1:
time: 40.3 us; the launch traced here: 39.8 us
  starting transfers between devices  18.2 us (45%)
  Pallas kernels  13.5 us (33%)
  waiting for transfers between devices  6.16 us (15%)
  local copies, waits for them, and re-layouts  1.08 us (3%)
  between operations  0.71 us (2%)
    pallas_call x10, Pallas kernels, call(): pl.pallas_call(body, out_shape=outs, in_specs=[VMEM] * len(args) + [pl.Bl...  13.5 us
    ppermute x2, starting transfers between devices, shards(): lax.ppermute(x, AXES, pairs)  5.18 us
    ppermute x1, starting transfers between devices, shards(): beside = lax.ppermute(own_ext, AXES, BESIDE)  5.16 us
    ppermute x1, starting transfers between devices, shards(): blocks.append(lax.ppermute(sent, AXES, SWAPS[2]))  3.28 us
    ppermute x1, starting transfers between devices, shards(): off = lax.ppermute(average, AXES, OFF_CHIP)  2.97 us
    ppermute x1, waiting for transfers between devices, shards(): blocks.append(lax.ppermute(sent, AXES, SWAPS[1]))  2.62 us
    ppermute x1, waiting for transfers between devices, shards(): beside = lax.ppermute(own_ext, AXES, BESIDE)  1.63 us
    ppermute x1, waiting for transfers between devices, shards(): exts = (pair, lax.ppermute(pair, AXES, OPPOSITE))  1.26 us
  transfers between devices with their start and end apart: 8, of which 4 were waited for; matrix products, arithmetic and copies ran while one was open for 0% of the time, Pallas kernels for 25%

profile of v1, /device:TPU:2, one launch (start us, length us, event | category | flops | bytes accessed | tf_op | source)
XLA Modules:
  0.0 39.8 jit_solution(8929426020835603487)
XLA Ops:
  0.6 0.0 copy-start.5
  0.6 0.0 copy-start.1
  0.7 2.4 %shard_map.123 = (f32[8,1280]{1,0:T(8,128)}, f32[8,1280]{1,0:T(8,128)}, f32[8,512]{1,0:T(8,128)}) custom-call(f32[72,512]{1,0:T(8,128)} %refs_0_.3, f32[72,512]{1,0:T(8,128)} %refs_3_.1, f32[1,512]{1,0:T(1,128)} %bitcast.7, f32[1,512]{1,0:T(1,128)} %bitcast.8, s32[1,512]{1,0:T(1,128)} %bitcast.9, s32[1,512]{1,0:T(1,128)} %bitcast.10, f32[1,512]{1,0:T(1,128)} %bitcast.11, ...), custom_call_target="tpu_custom_call" | custom-call | tf_op jit(solution)/shard_map/pallas_call | solution.py:411
  3.0 3.2 %collective-permute-start.2 = (f32[8,1280]{1,0:T(8,128)}, f32[8,1280]{1,0:T(8,128)S(1)}, u32[]{:S(2)}, u32[]{:S(2)}) collective-permute-start(f32[8,1280]{1,0:T(8,128)} %get-tuple-element.16), channel_id=1, source_target_pairs={{0,128},{1,64},{2,0},{3,192},{4,132},{5,68},{6,4},{7,196},{8,136},... | collective-permute-start | bytes 122888 | tf_op jit(solution)/shard_map/ppermute | solution.py:487
  6.3 1.9 %collective-permute-start.3 = (f32[8,1280]{1,0:T(8,128)}, f32[8,1280]{1,0:T(8,128)S(1)}, u32[]{:S(2)}, u32[]{:S(2)}) collective-permute-start(f32[8,1280]{1,0:T(8,128)} %get-tuple-element.17), channel_id=1, source_target_pairs={{0,160},{1,96},{2,32},{3,224},{4,164},{5,100},{6,36},{7,228},{8,16... | collective-permute-start | bytes 122888 | tf_op jit(solution)/shard_map/ppermute | solution.py:487
  8.2 0.0 copy-done.5
  8.2 0.1 copy.13
  8.3 0.0 copy-done.4
  8.3 0.1 select_maximum_fusion.refs_0_
  8.4 5.2 %collective-permute-start = (f32[16,128]{1,0:T(8,128)S(1)}, f32[16,128]{1,0:T(8,128)S(1)}, u32[]{:S(2)}, u32[]{:S(2)}) collective-permute-start(f32[16,128]{1,0:T(8,128)S(1)} %select_maximum_fusion.refs_0_), channel_id=1, source_target_pairs={{0,1},{1,0},{2,3},{3,2},{4,5},{5,4},{6,7},{7,6},{8,9},{9,8},{10,11... | collective-permute-start | bytes 24584 | tf_op jit(solution)/shard_map/ppermute | solution.py:488
  13.6 1.6 %collective-permute-done.refs_1_ = f32[16,128]{1,0:T(8,128)S(1)} collective-permute-done((f32[16,128]{1,0:T(8,128)S(1)}, f32[16,128]{1,0:T(8,128)S(1)}, u32[]{:S(2)}, u32[]{:S(2)}) %collective-permute-start) | collective-permute-done | bytes 8224 | tf_op jit(solution)/shard_map/ppermute | solution.py:488
  15.2 0.8 %collective-permute-start.1 = (f32[32,128]{1,0:T(8,128)S(1)}, f32[32,128]{1,0:T(8,128)S(1)}, u32[]{:S(2)}, u32[]{:S(2)}) collective-permute-start(f32[32,128]{1,0:T(8,128)S(1)} %shard_map.122.refs_3_.refs_0_), channel_id=1, source_target_pairs={{0,2},{1,3},{2,0},{3,1},{4,6},{5,7},{6,4},{7,5},{8,10},{9,11},{10,... | collective-permute-start | bytes 49160 | tf_op jit(solution)/shard_map/ppermute | solution.py:490
  16.0 0.0 copy-done.1
  16.0 0.0 copy-done.3
  16.0 1.0 %copy-done.2 = f32[2,72,512]{2,1,0:T(8,128)S(1)} copy-done((f32[2,72,512]{2,1,0:T(8,128)S(1)}, f32[2,72,512]{2,1,0:T(8,128)}, u32[]{:S(2)}) %copy-start.2) | copy-done | bytes 294936
  17.0 2.2 %shard_map.124 = (f32[72,512]{1,0:T(8,128)S(1)}, f32[72,512]{1,0:T(8,128)S(1)}, f32[72,512]{1,0:T(8,128)S(1)}, f32[3,72,512]{2,1,0:T(8,128)S(1)}, f32[72,128]{1,0:T(8,128)S(1)}, /*index=5*/bf16[128,512]{1,0:T(8,128)(2,1)S(1)}) custom-call(f32[8,512]{1,0:T(8,128)S(1)} %copy-done.3, f32[72,512]{1,0:T(8,128)S(1)} %copy-done.1, f32[2,72,512]{2,1,0:T(8,128)S(1)} %copy-done.2, ...), custom_call_target="tpu_custom_call" | custom-call | tf_op jit(solution)/shard_map/pallas_call | solution.py:411
  19.2 0.0 copy-start
  19.2 1.3 %collective-permute-done.1.refs_3_.refs_1_ = f32[32,128]{1,0:T(8,128)S(1)} collective-permute-done((f32[32,128]{1,0:T(8,128)S(1)}, f32[32,128]{1,0:T(8,128)S(1)}, u32[]{:S(2)}, u32[]{:S(2)}) %collective-permute-start.1) | collective-permute-done | bytes 16416 | tf_op jit(solution)/shard_map/ppermute | solution.py:490
  20.4 0.0 collective-permute-done.2.refs_0_.refs_2_
  20.4 0.0 collective-permute-done.3.refs_1_.refs_3_
  20.4 3.3 %collective-permute-start.4 = (f32[8,1280]{1,0:T(8,128)S(1)}, f32[8,1280]{1,0:T(8,128)S(1)}, u32[]{:S(2)}, u32[]{:S(2)}) collective-permute-start(f32[8,1280]{1,0:T(8,128)S(1)} %shard_map.125.refs_5_), channel_id=1, source_target_pairs={{0,16},{1,17},{2,18},{3,19},{4,20},{5,21},{6,22},{7,23},{8,24},{9,... | collective-permute-start | bytes 122888 | tf_op jit(solution)/shard_map/ppermute | solution.py:515
  23.7 3.7 %shard_map.126.refs_3_.refs_1_ = f32[72,512]{1,0:T(8,128)S(1)} custom-call(f32[32,128]{1,0:T(8,128)S(1)} %shard_map.122.refs_3_.refs_0_, f32[32,128]{1,0:T(8,128)S(1)} %collective-permute-done.1.refs_3_.refs_1_, f32[72,512]{1,0:T(8,128)S(1)} %copy-done, f32[72,512]{1,0:T(8,128)S(1)} %copy-done.1, f32[8,512]{1,0:T(8,128)S(1)} %copy-done.3, ...), custom_call_target="tpu_custom_call" | custom-call | tf_op jit(solution)/shard_map/pallas_call | solution.py:411
  27.5 0.0 collective-permute-done.4.refs_2_.refs_4_
  27.5 0.8 %collective-permute-start.5 = (f32[8,1280]{1,0:T(8,128)S(1)}, f32[8,1280]{1,0:T(8,128)S(1)}, u32[]{:S(2)}, u32[]{:S(2)}) collective-permute-start(f32[8,1280]{1,0:T(8,128)S(1)} %shard_map.127.refs_6_), channel_id=1, source_target_pairs={{0,8},{1,9},{2,10},{3,11},{4,12},{5,13},{6,14},{7,15},{8,0},{9,1},... | collective-permute-start | bytes 122888 | tf_op jit(solution)/shard_map/ppermute | solution.py:524
  28.3 0.7 %shard_map.128 = (f32[72,512]{1,0:T(8,128)S(1)}, f32[72,128]{1,0:T(8,128)S(1)}) custom-call(f32[72,512]{1,0:T(8,128)S(1)} %copy-done, f32[72,512]{1,0:T(8,128)S(1)} %shard_map.126.refs_3_.refs_1_, f32[72,512]{1,0:T(8,128)S(1)} %get-tuple-element.19.refs_2_, f32[72,512]{1,0:T(8,128)S(1)} %get-tuple-element.20.refs_3_, ...), custom_call_target="tpu_custom_call" | custom-call | tf_op jit(solution)/shard_map/pallas_call | solution.py:411
  29.0 2.6 %collective-permute-done.5.refs_3_.refs_5_ = f32[8,1280]{1,0:T(8,128)S(1)} collective-permute-done((f32[8,1280]{1,0:T(8,128)S(1)}, f32[8,1280]{1,0:T(8,128)S(1)}, u32[]{:S(2)}, u32[]{:S(2)}) %collective-permute-start.5) | collective-permute-done | bytes 40992 | tf_op jit(solution)/shard_map/ppermute | solution.py:524
  31.6 0.1 collective-permute-start.6
  31.7 3.0 %collective-permute-start.7 = (f32[72,128]{1,0:T(8,128)S(1)}, f32[72,128]{1,0:T(8,128)S(1)}, u32[]{:S(2)}, u32[]{:S(2)}) collective-permute-start(f32[72,128]{1,0:T(8,128)S(1)} %get-tuple-element.24.refs_4_.refs_2_), channel_id=1, source_target_pairs={{0,252},{1,253},{2,254},{3,255},{4,8},{5,9},{6,10},{7,11},{8,4},{9... | collective-permute-start | bytes 110600 | tf_op jit(solution)/shard_map/ppermute | solution.py:532
  34.7 0.0 collective-permute-done.6.refs_6_.refs_3_
  34.7 3.2 %shard_map.130 = (f32[72,256]{1,0:T(8,128)}, f32[8,128]{1,0:T(8,128)S(1)}) custom-call(f32[32,128]{1,0:T(8,128)S(1)} %shard_map.122.refs_3_.refs_0_, f32[32,128]{1,0:T(8,128)S(1)} %collective-permute-done.1.refs_3_.refs_1_, f32[8,1280]{1,0:T(8,128)S(1)} %collective-permute-done.2.refs_0_.refs_2_, f32[8,1280]{1,0:T(8,128)S(1)} %collective-permute-done.3.refs_1_.refs_3_, ...), custom_call_target="tpu_custom_call" | custom-call | tf_op jit(solution)/shard_map/pallas_call | solution.py:411
  37.9 0.6 %collective-permute-done.7.refs_4_ = f32[72,128]{1,0:T(8,128)S(1)} collective-permute-done((f32[72,128]{1,0:T(8,128)S(1)}, f32[72,128]{1,0:T(8,128)S(1)}, u32[]{:S(2)}, u32[]{:S(2)}) %collective-permute-start.7) | collective-permute-done | bytes 36896 | tf_op jit(solution)/shard_map/ppermute | solution.py:532
  38.5 1.3 %shard_map.131 = f32[4,72,512]{2,1,0:T(8,128)} custom-call(f32[72,512]{1,0:T(8,128)S(1)} %get-tuple-element.22.refs_0_, f32[3,72,512]{2,1,0:T(8,128)S(1)} %get-tuple-element.23.refs_1_, f32[72,128]{1,0:T(8,128)S(1)} %get-tuple-element.24.refs_4_.refs_2_, f32[8,2432]{1,0:T(8,128)S(1)} %collective-permute-done.6.refs_6_.refs_3_, ...), custom_call_target="tpu_custom_call" | custom-call | tf_op jit(solution)/shard_map/pallas_call | solution.py:411
  (8 shorter events, 0.1 us)
Async XLA Ops:
  0.6 7.6 %copy-start.5 = (f32[14]{0:T(128)S(1)}, f32[14]{0:T(128)}, u32[]{:S(2)}) copy-start(f32[14]{0:T(128)} %param.21) | copy-start | bytes 172
  0.6 15.3 %copy-start.1 = (f32[72,512]{1,0:T(8,128)S(1)}, f32[72,512]{1,0:T(8,128)}, u32[]{:S(2)}) copy-start(f32[72,512]{1,0:T(8,128)} %refs_3_.1) | copy-start | bytes 442372
  3.0 5.3 %copy-start.4 = (f32[14,72]{1,0:T(8,128)S(1)}, f32[14,72]{1,0:T(8,128)}, u32[]{:S(2)}) copy-start(f32[14,72]{1,0:T(8,128)} %param.20) | copy-start | bytes 12100
  3.0 17.4 %collective-permute-start.2 = (f32[8,1280]{1,0:T(8,128)}, f32[8,1280]{1,0:T(8,128)S(1)}, u32[]{:S(2)}, u32[]{:S(2)}) collective-permute-start(f32[8,1280]{1,0:T(8,128)} %get-tuple-element.16), channel_id=1, source_target_pairs={{0,128},{1,64},{2,0},{3,192},{4,132},{5,68},{6,4},{7,196},{8,136},... | collective-permute-start | bytes 122888 | tf_op jit(solution)/shard_map/ppermute | solution.py:487
  6.3 14.2 %collective-permute-start.3 = (f32[8,1280]{1,0:T(8,128)}, f32[8,1280]{1,0:T(8,128)S(1)}, u32[]{:S(2)}, u32[]{:S(2)}) collective-permute-start(f32[8,1280]{1,0:T(8,128)} %get-tuple-element.17), channel_id=1, source_target_pairs={{0,160},{1,96},{2,32},{3,224},{4,164},{5,100},{6,36},{7,228},{8,16... | collective-permute-start | bytes 122888 | tf_op jit(solution)/shard_map/ppermute | solution.py:487
  8.4 7.6 %copy-start.3 = (f32[8,512]{1,0:T(8,128)S(1)}, f32[8,512]{1,0:T(8,128)}, u32[]{:S(2)}) copy-start(f32[8,512]{1,0:T(8,128)} %get-tuple-element.15.refs_0_.refs_4_) | copy-start | bytes 49156
  8.4 6.8 %collective-permute-start = (f32[16,128]{1,0:T(8,128)S(1)}, f32[16,128]{1,0:T(8,128)S(1)}, u32[]{:S(2)}, u32[]{:S(2)}) collective-permute-start(f32[16,128]{1,0:T(8,128)S(1)} %select_maximum_fusion.refs_0_), channel_id=1, source_target_pairs={{0,1},{1,0},{2,3},{3,2},{4,5},{5,4},{6,7},{7,6},{8,9},{9,8},{10,11... | collective-permute-start | bytes 24584 | tf_op jit(solution)/shard_map/ppermute | solution.py:488
  15.2 5.2 %collective-permute-start.1 = (f32[32,128]{1,0:T(8,128)S(1)}, f32[32,128]{1,0:T(8,128)S(1)}, u32[]{:S(2)}, u32[]{:S(2)}) collective-permute-start(f32[32,128]{1,0:T(8,128)S(1)} %shard_map.122.refs_3_.refs_0_), channel_id=1, source_target_pairs={{0,2},{1,3},{2,0},{3,1},{4,6},{5,7},{6,4},{7,5},{8,10},{9,11},{10,... | collective-permute-start | bytes 49160 | tf_op jit(solution)/shard_map/ppermute | solution.py:490
  16.0 1.0 %copy-start.2 = (f32[2,72,512]{2,1,0:T(8,128)S(1)}, f32[2,72,512]{2,1,0:T(8,128)}, u32[]{:S(2)}) copy-start(f32[2,72,512]{2,1,0:T(8,128)} %refs_2_.2) | copy-start | bytes 884740
  19.2 4.6 %copy-start = (f32[72,512]{1,0:T(8,128)S(1)}, f32[72,512]{1,0:T(8,128)}, u32[]{:S(2)}) copy-start(f32[72,512]{1,0:T(8,128)} %refs_0_.3) | copy-start | bytes 442372
  20.4 7.0 %collective-permute-start.4 = (f32[8,1280]{1,0:T(8,128)S(1)}, f32[8,1280]{1,0:T(8,128)S(1)}, u32[]{:S(2)}, u32[]{:S(2)}) collective-permute-start(f32[8,1280]{1,0:T(8,128)S(1)} %shard_map.125.refs_5_), channel_id=1, source_target_pairs={{0,16},{1,17},{2,18},{3,19},{4,20},{5,21},{6,22},{7,23},{8,24},{9,... | collective-permute-start | bytes 122888 | tf_op jit(solution)/shard_map/ppermute | solution.py:515
  27.5 4.1 %collective-permute-start.5 = (f32[8,1280]{1,0:T(8,128)S(1)}, f32[8,1280]{1,0:T(8,128)S(1)}, u32[]{:S(2)}, u32[]{:S(2)}) collective-permute-start(f32[8,1280]{1,0:T(8,128)S(1)} %shard_map.127.refs_6_), channel_id=1, source_target_pairs={{0,8},{1,9},{2,10},{3,11},{4,12},{5,13},{6,14},{7,15},{8,0},{9,1},... | collective-permute-start | bytes 122888 | tf_op jit(solution)/shard_map/ppermute | solution.py:524
  31.6 3.1 %collective-permute-start.6 = (f32[8,2432]{1,0:T(8,128)S(1)}, f32[8,2432]{1,0:T(8,128)S(1)}, u32[]{:S(2)}, u32[]{:S(2)}) collective-permute-start(f32[8,2432]{1,0:T(8,128)S(1)} %shard_map.129), channel_id=1, source_target_pairs={{0,4},{1,5},{2,6},{3,7},{4,0},{5,1},{6,2},{7,3},{8,12},{9,13},{10,... | collective-permute-start | bytes 233480 | tf_op jit(solution)/shard_map/ppermute | solution.py:534
  31.7 6.8 %collective-permute-start.7 = (f32[72,128]{1,0:T(8,128)S(1)}, f32[72,128]{1,0:T(8,128)S(1)}, u32[]{:S(2)}, u32[]{:S(2)}) collective-permute-start(f32[72,128]{1,0:T(8,128)S(1)} %get-tuple-element.24.refs_4_.refs_2_), channel_id=1, source_target_pairs={{0,252},{1,253},{2,254},{3,255},{4,8},{5,9},{6,10},{7,11},{8,4},{9... | collective-permute-start | bytes 110600 | tf_op jit(solution)/shard_map/ppermute | solution.py:532

commit v2 on v1

--- a/solution.py
+++ b/solution.py
@@ -84,8 +84,8 @@
         gone = gone + jnp.sum(onehot, axis=1, keepdims=True)
     rank = jnp.concatenate(ranks, axis=1).astype(jnp.int32)
     sent = ((dest >> 4) == served) & (lit_ref[...] != 0)
-    apart = (dest ^ lax.axis_index("elem")) & 15
-    slot = jnp.where(sent, apart * 16 + rank, -1)
+    apart = (dest ^ lax.axis_index("elem") ^ 1) & 15
+    slot = jnp.where(sent, coded(apart) * 16 + rank, -1)
     chosen = jnp.where(slot == iota((256, COLS), 0), 1.0, 0.0).astype(BF16)
     row = iota((8, COLS), 0)
     tail = jnp.where(row == 0, mu_ref[...], jnp.where(row == 1, albedo_ref[...], 0.0))
@@ -102,6 +102,10 @@
             out_ref[:, at] = swap_groups(part)
 
 
+def coded(apart):
+    return apart ^ (((apart >> 1) ^ (apart >> 2)) & 1)
+
+
 def bit_of_row(bit):
     return (iota((8, WIDE), 0) >> bit) & 1
 
@@ -120,11 +124,6 @@
     for bit, got in zip((2, 1, 0), blocks[2:]):
         low, high = put(low, high, got[...], bit)
     return low, high
-
-
-def pair_kernel(own_ref, beside_ref, exts_ref):
-    exts_ref[:16] = own_ref[...]
-    exts_ref[16:] = beside_ref[...]
 
 
 def next_kernel(*refs):
@@ -206,9 +205,8 @@
 
 
 def load_extinction(blocks, ext_ref):
-    for k in range(4):
-        at = 16 * (k & 1)
-        ext_ref[14 * k : 14 * k + 14] = blocks[k >> 1][at : at + 14] * SCALE
+    for k, block in enumerate(blocks):
+        ext_ref[14 * k : 14 * k + 14] = block[:14] * SCALE
 
 
 def octet(count):
@@ -250,9 +248,88 @@
 
 def factor_kernel(
     scalar_ref, q_ref, wind_ref,
-    inv_ref, down_ref, ratio_ref, tend_ref, avg_ref, correct_ref,
+    inv_ref, down_ref, ratio_ref, tend_ref,
     upper_ref, lower_ref, value_ref,
 ):
+    u, v = wind_ref[0], wind_ref[1]
+    mix = scalar_ref[STRENGTH : STRENGTH + 1] * (1.0 + ((u[:-1] - u[1:]) ** 2 + (v[:-1] - v[1:]) ** 2))
+    edge = jnp.zeros((1, COLS), F32)
+    upper_ref[...] = jnp.concatenate([edge, mix], axis=0)
+    lower_ref[...] = jnp.concatenate([mix, edge], axis=0)
+
+    def forward(carried, upper, lower, *sides):
+        ratio, values = carried
+        inverse = 1.0 / ((1.0 + upper + lower) - upper * ratio)
+        ratio = lower * inverse
+        down = upper * inverse
+        values = [side * inverse + down * value for side, value in zip(sides, values)]
+        return (ratio, values), (inverse, down, ratio, *values)
+
+    zero = jnp.zeros((8, COLS), F32)
+    sides = [reader(q_ref), reader(wind_ref, 0), reader(wind_ref, 1)]
+    sweep(
+        (
+            [reader(upper_ref), reader(lower_ref), *sides],
+            [writer(inv_ref), writer(down_ref), writer(ratio_ref)]
+            + [writer(value_ref, f) for f in range(3)],
+        ),
+        forward,
+        (zero, [zero] * 3),
+    )
+
+    def backward(solved, ratio, *values):
+        solved = [value + ratio * x for value, x in zip(values, solved)]
+        return solved, solved
+
+    sweep(
+        (
+            [reader(ratio_ref)] + [reader(value_ref, f) for f in range(3)],
+            [writer(value_ref, f) for f in range(3)],
+        ),
+        backward,
+        [zero] * 3,
+        True,
+    )
+    tend_ref[0] = value_ref[0] - q_ref[...]
+    tend_ref[1:3] = value_ref[1:3] - wind_ref[...]
+
+
+def home_kernel(
+    e0, e1, e2, e3, t_ref, q_ref, scalar_ref, out_ref, a_ref, ext_ref, weight_ref, surface_ref
+):
+    load_extinction((e0, e1, e2, e3), ext_ref)
+    a_ref[...] = t_ref[...] * q_ref[...]
+    mu, albedo = scalar_ref[MU : MU + 1], scalar_ref[ALBEDO : ALBEDO + 1]
+    heat_columns(a_ref, out_ref, ext_ref, weight_ref, surface_ref, mu, albedo, 4)
+    out_ref[...] = out_ref[...] * scalar_ref[LIT : LIT + 1]
+
+
+def solve_kernel(
+    t_ref, flux_ref, inv_ref, down_ref, ratio_ref, late_ref, scalar_ref,
+    tend_ref, avg_ref, correct_ref,
+    heat_ref,
+):
+    side = t_ref[...] + flux_ref[...]
+    heat_ref[...] = side * inv_ref[...]
+
+    def forward(value, side, down):
+        value = side + down * value
+        return value, (value,)
+
+    def backward(solved, value, ratio):
+        solved = value + ratio * solved
+        return solved, (solved,)
+
+    zero = jnp.zeros((8, COLS), F32)
+    writes = [writer(heat_ref)]
+    sweep(([reader(heat_ref), reader(down_ref)], writes), forward, zero)
+    sweep(([reader(heat_ref), reader(ratio_ref)], writes), backward, zero, True)
+    tend = heat_ref[...] - t_ref[...]
+    tend_ref[...] = tend
+    avg = times(tend, element_mean(0))
+    for f in range(3):
+        avg = avg + times(late_ref[f], element_mean(f + 1))
+    avg_ref[...] = avg
     spread = jnp.where(iota((32, COLS), 0) == (iota((32, COLS), 1) >> 4), 1.0, 0.0).astype(BF16)
     row = iota((LANES, COLS), 0)
     weight = jnp.where(row == 32 + (iota((LANES, COLS), 1) >> 4), -2.0, 0.0)
@@ -264,93 +341,20 @@
     for k in range(4):
         weight = weight + jnp.where(row == local[k : k + 1], 0.5, 0.0)
     correct_ref[...] = weight.astype(BF16)
-    u, v = wind_ref[0], wind_ref[1]
-    mix = scalar_ref[STRENGTH : STRENGTH + 1] * (1.0 + ((u[:-1] - u[1:]) ** 2 + (v[:-1] - v[1:]) ** 2))
-    edge = jnp.zeros((1, COLS), F32)
-    upper_ref[...] = jnp.concatenate([edge, mix], axis=0)
-    lower_ref[...] = jnp.concatenate([mix, edge], axis=0)
-
-    def forward(carried, upper, lower, *sides):
-        ratio, values = carried
-        inverse = 1.0 / ((1.0 + upper + lower) - upper * ratio)
-        ratio = lower * inverse
-        down = upper * inverse
-        values = [side * inverse + down * value for side, value in zip(sides, values)]
-        return (ratio, values), (inverse, down, ratio, *values)
-
-    zero = jnp.zeros((8, COLS), F32)
-    sides = [reader(q_ref), reader(wind_ref, 0), reader(wind_ref, 1)]
-    sweep(
-        (
-            [reader(upper_ref), reader(lower_ref), *sides],
-            [writer(inv_ref), writer(down_ref), writer(ratio_ref)]
-            + [writer(value_ref, f) for f in range(3)],
-        ),
-        forward,
-        (zero, [zero] * 3),
-    )
-
-    def backward(solved, ratio, *values):
-        solved = [value + ratio * x for value, x in zip(values, solved)]
-        return solved, solved
-
-    sweep(
-        (
-            [reader(ratio_ref)] + [reader(value_ref, f) for f in range(3)],
-            [writer(value_ref, f) for f in range(3)],
-        ),
-        backward,
-        [zero] * 3,
-        True,
-    )
-    tend_ref[0] = value_ref[0] - q_ref[...]
-    tend_ref[1:3] = value_ref[1:3] - wind_ref[...]
-    avg = jnp.zeros((LEVELS, LANES), F32)
-    for f in range(3):
-        avg = avg + times(tend_ref[f], element_mean(f + 1))
-    avg_ref[...] = avg
-
-
-def home_kernel(
-    e0, e1, t_ref, q_ref, scalar_ref, out_ref, a_ref, ext_ref, weight_ref, surface_ref
-):
-    load_extinction((e0, e1), ext_ref)
-    a_ref[...] = t_ref[...] * q_ref[...]
-    mu, albedo = scalar_ref[MU : MU + 1], scalar_ref[ALBEDO : ALBEDO + 1]
-    heat_columns(a_ref, out_ref, ext_ref, weight_ref, surface_ref, mu, albedo, 4)
-    out_ref[...] = out_ref[...] * scalar_ref[LIT : LIT + 1]
-
-
-def solve_kernel(t_ref, flux_ref, inv_ref, down_ref, ratio_ref, early_ref, tend_ref, avg_ref, heat_ref):
-    side = t_ref[...] + flux_ref[...]
-    heat_ref[...] = side * inv_ref[...]
-
-    def forward(value, side, down):
-        value = side + down * value
-        return value, (value,)
-
-    def backward(solved, value, ratio):
-        solved = value + ratio * solved
-        return solved, (solved,)
-
-    zero = jnp.zeros((8, COLS), F32)
-    writes = [writer(heat_ref)]
-    sweep(([reader(heat_ref), reader(down_ref)], writes), forward, zero)
-    sweep(([reader(heat_ref), reader(ratio_ref)], writes), backward, zero, True)
-    tend = heat_ref[...] - t_ref[...]
-    tend_ref[...] = tend
-    avg_ref[...] = early_ref[...] + times(tend, element_mean(0))
 
 
 def span_kernel(
-    e0, e1, b0, b1, b2, b3, last_ref, out_ref, token_ref,
+    e0, e1, e2, e3, b0, b1, b2, b3, last_ref, out_ref, token_ref,
     a_ref, heat_ref, ext_ref, weight_ref, surface_ref,
 ):
-    load_extinction((e0, e1), ext_ref)
-    place = lax.axis_index("elem")
+    load_extinction((e0, e1, e2, e3), ext_ref)
+    place = lax.axis_index("elem") ^ 1
     halves = list(held((b0, b1, b2, b3, last_ref.at[:, :WIDE])))
+    mixed = (bit_of_row(1) ^ bit_of_row(2)) & 1
     for bit in range(3):
         turn = ((place >> bit) & 1) == 1
+        if bit == 0:
+            turn = ((place & 1) ^ mixed) == 1
         height = 1 << bit
         clear = bit_of_row(bit) == 0
         halves = [
@@ -426,11 +430,13 @@
     return 4 * s + m
 
 
-BESIDE = [(number(s, m), number(s, m ^ 1)) for s in range(64) for m in range(4)]
-OPPOSITE = [(number(s, m), number(s, m ^ 2)) for s in range(64) for m in range(4)]
+ASIDE = [
+    [(number(s, m), number(s ^ 1, m ^ move)) for s in range(64) for m in range(4)]
+    for move in (1, 2, 3)
+]
 SWAPS = [
-    [(number(s, m), number(s ^ (1 << bit), m)) for s in range(64) for m in range(4)]
-    for bit in range(4)
+    [(number(s, m), number(s ^ move, m)) for s in range(64) for m in range(4)]
+    for move in (1, 3, 5)
 ]
 ACROSS = [
     [
@@ -439,7 +445,7 @@
         for i in range(16)
         for m in range(4)
     ]
-    for flip in (0, 8)
+    for flip in (1, 9)
 ]
 OFF_CHIP = [
     (number(s, m), number((s - 1 if s % 2 == 0 else s + 1) % 64, m))
@@ -485,14 +491,11 @@
         limit=60,
     )
     blocks = [lax.ppermute(x, AXES, pairs) for x, pairs in zip((low, high), ACROSS)]
-    beside = lax.ppermute(own_ext, AXES, BESIDE)
-    pair = call(pair_kernel, shape(32, LANES), [], own_ext, beside)
-    exts = (pair, lax.ppermute(pair, AXES, OPPOSITE))
-    inverse, down, ratio, tend_late, early, correct = call(
+    exts = [own_ext] + [lax.ppermute(own_ext, AXES, pairs) for pairs in ASIDE]
+    inverse, down, ratio, tend_late = call(
         factor_kernel,
         [
-            field, field, field, shape(3, LEVELS, COLS), shape(LEVELS, LANES),
-            shape(LANES, COLS, dtype=BF16),
+            field, field, field, shape(3, LEVELS, COLS),
         ],
         [
             *[pltpu.VMEM((LEVELS, COLS), F32)] * 2,
@@ -501,7 +504,6 @@
         scalars,
         moisture_content,
         lateral_velocity_components,
-        after=(pair,),
     )
 
     def tables(columns):
@@ -511,7 +513,7 @@
             pltpu.VMEM((56, columns), F32),
         ]
 
-    sent = call(next_kernel, message, [], *blocks, after=(early, exts[1]))
+    sent = call(next_kernel, message, [], *blocks, after=(ratio, *exts[1:]))
     blocks.append(lax.ppermute(sent, AXES, SWAPS[2]))
     heat = call(
         home_kernel,
@@ -522,11 +524,11 @@
     )
     sent = call(next_kernel, message, [], *blocks, after=(heat,))
     blocks.append(lax.ppermute(sent, AXES, SWAPS[1]))
-    tend0, average = call(
+    tend0, average, correct = call(
         solve_kernel,
-        [field, shape(LEVELS, LANES)],
+        [field, shape(LEVELS, LANES), shape(LANES, COLS, dtype=BF16)],
         [pltpu.VMEM((LEVELS, COLS), F32)],
-        thermal_state, heat, inverse, down, ratio, early,
+        thermal_state, heat, inverse, down, ratio, tend_late, scalars,
         after=(sent,),
     )
     off = lax.ppermute(average, AXES, OFF_CHIP)

time: 40.3 us -> 37.3 us (0.926)
  waiting for transfers between devices: 6.16 us -> 3.31 us
  starting transfers between devices: 18.2 us -> 18.7 us
    ppermute x2 -> x3, waiting for transfers between devices: 2.89 us -> 0.63 us  [shards(): exts = [own_ext] + [lax.ppermute(own_ext, AXES, pairs) for pairs in ASIDE]]
    ppermute x2 -> x3, starting transfers between devices: 5.96 us -> 6.94 us  [shards(): exts = [own_ext] + [lax.ppermute(own_ext, AXES, pairs) for pairs in ASIDE]]
    ppermute x1, waiting for transfers between devices: 2.62 us -> 1.7 us  [shards(): blocks.append(lax.ppermute(sent, AXES, SWAPS[1]))]
    ppermute x1, starting transfers between devices: 2.97 us -> 2.54 us  [shards(): off = lax.ppermute(average, AXES, OFF_CHIP)]
    ppermute x1, starting transfers between devices: 0.09 us -> 0.52 us  [shards(): last = lax.ppermute(sent, AXES, SWAPS[0])]
    pallas_call x10 -> x9, Pallas kernels: 13.5 us -> 13.2 us  [call(): pl.pallas_call(body, out_shape=outs, in_specs=[VMEM] * len(args) + [pl.Bl...]
  transfers between devices with their start and end apart: 8 -> 9, of which waited for: 4 -> 3; matrix products, arithmetic and copies ran while one was open for 0% -> 0% of each run, Pallas kernels for 25% -> 26%
where the time goes in v2:
time: 37.3 us; the launch traced here: 37.1 us
  starting transfers between devices  18.7 us (50%)
  Pallas kernels  13.2 us (35%)
  waiting for transfers between devices  3.31 us (9%)
  local copies, waits for them, and re-layouts  1.07 us (3%)
  between operations  0.74 us (2%)
    pallas_call x9, Pallas kernels, call(): pl.pallas_call(body, out_shape=outs, in_specs=[VMEM] * len(args) + [pl.Bl...  13.2 us
    ppermute x3, starting transfers between devices, shards(): exts = [own_ext] + [lax.ppermute(own_ext, AXES, pairs) for pairs in ASIDE]  6.94 us
    ppermute x2, starting transfers between devices, shards(): lax.ppermute(x, AXES, pairs)  4.9 us
    ppermute x1, starting transfers between devices, shards(): blocks.append(lax.ppermute(sent, AXES, SWAPS[2]))  3 us
    ppermute x1, starting transfers between devices, shards(): off = lax.ppermute(average, AXES, OFF_CHIP)  2.54 us
    ppermute x1, waiting for transfers between devices, shards(): blocks.append(lax.ppermute(sent, AXES, SWAPS[1]))  1.7 us
    unnamed x12, local copies, waits for them, and re-layouts  0.98 us
    ppermute x1, waiting for transfers between devices, shards(): off = lax.ppermute(average, AXES, OFF_CHIP)  0.97 us
  transfers between devices with their start and end apart: 9, of which 3 were waited for; matrix products, arithmetic and copies ran while one was open for 0% of the time, Pallas kernels for 26%

profile of v2, /device:TPU:2, one launch (start us, length us, event | category | flops | bytes accessed | tf_op | source)
XLA Modules:
  0.0 37.1 jit_solution(13906450688569775002)
XLA Ops:
  0.6 0.0 copy-start.5
  0.6 0.0 copy-start.1
  0.7 2.4 %shard_map.122 = (f32[8,1280]{1,0:T(8,128)}, f32[8,1280]{1,0:T(8,128)}, f32[8,512]{1,0:T(8,128)}) custom-call(f32[72,512]{1,0:T(8,128)} %refs_0_.3, f32[72,512]{1,0:T(8,128)} %refs_5_.1, f32[1,512]{1,0:T(1,128)} %bitcast.7, f32[1,512]{1,0:T(1,128)} %bitcast.8, s32[1,512]{1,0:T(1,128)} %bitcast.9, s32[1,512]{1,0:T(1,128)} %bitcast.10, f32[1,512]{1,0:T(1,128)} %bitcast.11, ...), custom_call_target="tpu_custom_call" | custom-call | tf_op jit(solution)/shard_map/pallas_call | solution.py:415
  3.0 2.7 %collective-permute-start.3 = (f32[8,1280]{1,0:T(8,128)}, f32[8,1280]{1,0:T(8,128)S(1)}, u32[]{:S(2)}, u32[]{:S(2)}) collective-permute-start(f32[8,1280]{1,0:T(8,128)} %get-tuple-element.15), channel_id=1, source_target_pairs={{0,132},{1,68},{2,4},{3,196},{4,128},{5,64},{6,0},{7,192},{8,140},... | collective-permute-start | bytes 122888 | tf_op jit(solution)/shard_map/ppermute | solution.py:493
  5.7 2.2 %collective-permute-start.4 = (f32[8,1280]{1,0:T(8,128)}, f32[8,1280]{1,0:T(8,128)S(1)}, u32[]{:S(2)}, u32[]{:S(2)}) collective-permute-start(f32[8,1280]{1,0:T(8,128)} %get-tuple-element.16), channel_id=1, source_target_pairs={{0,164},{1,100},{2,36},{3,228},{4,160},{5,96},{6,32},{7,224},{8,17... | collective-permute-start | bytes 122888 | tf_op jit(solution)/shard_map/ppermute | solution.py:493
  7.9 0.0 copy-done.5
  7.9 0.1 copy.13
  8.0 0.1 select_maximum_fusion.refs_0_
  8.1 3.9 %collective-permute-start.2 = (f32[16,128]{1,0:T(8,128)S(1)}, f32[16,128]{1,0:T(8,128)S(1)}, u32[]{:S(2)}, u32[]{:S(2)}) collective-permute-start(f32[16,128]{1,0:T(8,128)S(1)} %select_maximum_fusion.refs_0_), channel_id=1, source_target_pairs={{0,7},{1,6},{2,5},{3,4},{4,3},{5,2},{6,1},{7,0},{8,15},{9,14},{10,... | collective-permute-start | bytes 24584 | tf_op jit(solution)/shard_map/ppermute | solution.py:494
  12.0 3.0 %collective-permute-start.1 = (f32[16,128]{1,0:T(8,128)S(1)}, f32[16,128]{1,0:T(8,128)S(1)}, u32[]{:S(2)}, u32[]{:S(2)}) collective-permute-start(f32[16,128]{1,0:T(8,128)S(1)} %select_maximum_fusion.refs_0_), channel_id=1, source_target_pairs={{0,6},{1,7},{2,4},{3,5},{4,2},{5,3},{6,0},{7,1},{8,14},{9,15},{10,... | collective-permute-start | bytes 24584 | tf_op jit(solution)/shard_map/ppermute | solution.py:494
  15.1 0.0 collective-permute-start
  15.1 0.0 copy-done.3
  15.1 0.0 copy-start.2
  15.1 1.0 %copy-done.2 = f32[2,72,512]{2,1,0:T(8,128)S(1)} copy-done((f32[2,72,512]{2,1,0:T(8,128)S(1)}, f32[2,72,512]{2,1,0:T(8,128)}, u32[]{:S(2)}) %copy-start.2) | copy-done | bytes 294936
  16.0 1.5 %shard_map.123 = (f32[72,512]{1,0:T(8,128)S(1)}, f32[72,512]{1,0:T(8,128)S(1)}, f32[72,512]{1,0:T(8,128)S(1)}, f32[3,72,512]{2,1,0:T(8,128)S(1)}) custom-call(f32[8,512]{1,0:T(8,128)S(1)} %copy-done.3, f32[72,512]{1,0:T(8,128)S(1)} %copy-done.1, f32[2,72,512]{2,1,0:T(8,128)S(1)} %copy-done.2), custom_call_target="tpu_custom_call" | custom-call | tf_op jit(solution)/shard_map/pallas_call | solution.py:415
  17.6 0.0 collective-permute-done.2.refs_5_.refs_3_
  17.6 0.0 collective-permute-done.1.refs_4_.refs_2_
  17.6 0.6 %collective-permute-done.refs_3_.refs_1_ = f32[16,128]{1,0:T(8,128)S(1)} collective-permute-done((f32[16,128]{1,0:T(8,128)S(1)}, f32[16,128]{1,0:T(8,128)S(1)}, u32[]{:S(2)}, u32[]{:S(2)}) %collective-permute-start) | collective-permute-done | bytes 8224 | tf_op jit(solution)/shard_map/ppermute | solution.py:494
  18.2 0.0 collective-permute-done.3.refs_0_.refs_4_
  18.2 0.0 collective-permute-done.4.refs_1_.refs_5_
  18.2 3.0 %collective-permute-start.5 = (f32[8,1280]{1,0:T(8,128)S(1)}, f32[8,1280]{1,0:T(8,128)S(1)}, u32[]{:S(2)}, u32[]{:S(2)}) collective-permute-start(f32[8,1280]{1,0:T(8,128)S(1)} %shard_map.124.refs_7_), channel_id=1, source_target_pairs={{0,20},{1,21},{2,22},{3,23},{4,16},{5,17},{6,18},{7,19},{8,28},{9,... | collective-permute-start | bytes 122888 | tf_op jit(solution)/shard_map/ppermute | solution.py:517
  21.2 3.7 %shard_map.125.refs_3_.refs_1_ = f32[72,512]{1,0:T(8,128)S(1)} custom-call(f32[16,128]{1,0:T(8,128)S(1)} %select_maximum_fusion.refs_0_, f32[16,128]{1,0:T(8,128)S(1)} %collective-permute-done.refs_3_.refs_1_, f32[16,128]{1,0:T(8,128)S(1)} %collective-permute-done.1.refs_4_.refs_2_, f32[16,128]{1,0:T(8,128)S(1)} %collective-permute-done.2.refs_5_.refs_3_, ...), custom_call_target="tpu_custom_call" | custom-call | tf_op jit(solution)/shard_map/pallas_call | solution.py:415
  25.0 0.0 collective-permute-done.5.refs_2_.refs_6_
  25.0 0.8 %collective-permute-start.6 = (f32[8,1280]{1,0:T(8,128)S(1)}, f32[8,1280]{1,0:T(8,128)S(1)}, u32[]{:S(2)}, u32[]{:S(2)}) collective-permute-start(f32[8,1280]{1,0:T(8,128)S(1)} %shard_map.126.refs_7_), channel_id=1, source_target_pairs={{0,12},{1,13},{2,14},{3,15},{4,8},{5,9},{6,10},{7,11},{8,4},{9,5},... | collective-permute-start | bytes 122888 | tf_op jit(solution)/shard_map/ppermute | solution.py:526
  25.8 1.0 %shard_map.127 = (f32[72,512]{1,0:T(8,128)S(1)}, f32[72,128]{1,0:T(8,128)S(1)}, bf16[128,512]{1,0:T(8,128)(2,1)S(1)}) custom-call(f32[72,512]{1,0:T(8,128)S(1)} %copy-done, f32[72,512]{1,0:T(8,128)S(1)} %shard_map.125.refs_3_.refs_1_, f32[72,512]{1,0:T(8,128)S(1)} %get-tuple-element.18.refs_2_, f32[72,512]{1,0:T(8,128)S(1)} %get-tuple-element.19.refs_3_, ...), custom_call_target="tpu_custom_call" | custom-call | tf_op jit(solution)/shard_map/pallas_call | solution.py:415
  26.8 1.7 %collective-permute-done.6.refs_3_.refs_7_ = f32[8,1280]{1,0:T(8,128)S(1)} collective-permute-done((f32[8,1280]{1,0:T(8,128)S(1)}, f32[8,1280]{1,0:T(8,128)S(1)}, u32[]{:S(2)}, u32[]{:S(2)}) %collective-permute-start.6) | collective-permute-done | bytes 40992 | tf_op jit(solution)/shard_map/ppermute | solution.py:526
  28.6 0.5 %collective-permute-start.7 = (f32[8,2432]{1,0:T(8,128)S(1)}, f32[8,2432]{1,0:T(8,128)S(1)}, u32[]{:S(2)}, u32[]{:S(2)}) collective-permute-start(f32[8,2432]{1,0:T(8,128)S(1)} %shard_map.128), channel_id=1, source_target_pairs={{0,4},{1,5},{2,6},{3,7},{4,0},{5,1},{6,2},{7,3},{8,12},{9,13},{10,... | collective-permute-start | bytes 233480 | tf_op jit(solution)/shard_map/ppermute | solution.py:536
  29.1 2.5 %collective-permute-start.8 = (f32[72,128]{1,0:T(8,128)S(1)}, f32[72,128]{1,0:T(8,128)S(1)}, u32[]{:S(2)}, u32[]{:S(2)}) collective-permute-start(f32[72,128]{1,0:T(8,128)S(1)} %get-tuple-element.22.refs_4_.refs_2_), channel_id=1, source_target_pairs={{0,252},{1,253},{2,254},{3,255},{4,8},{5,9},{6,10},{7,11},{8,4},{9... | collective-permute-start | bytes 110600 | tf_op jit(solution)/shard_map/ppermute | solution.py:534
  31.6 0.0 collective-permute-done.7.refs_8_.refs_3_
  31.6 3.2 %shard_map.129 = (f32[72,256]{1,0:T(8,128)}, f32[8,128]{1,0:T(8,128)S(1)}) custom-call(f32[16,128]{1,0:T(8,128)S(1)} %select_maximum_fusion.refs_0_, f32[16,128]{1,0:T(8,128)S(1)} %collective-permute-done.refs_3_.refs_1_, f32[16,128]{1,0:T(8,128)S(1)} %collective-permute-done.1.refs_4_.refs_2_, f32[16,128]{1,0:T(8,128)S(1)} %collective-permute-done.2.refs_5_.refs_3_, ...), custom_call_target="tpu_custom_call" | custom-call | tf_op jit(solution)/shard_map/pallas_call | solution.py:415
  34.8 1.0 %collective-permute-done.8.refs_4_ = f32[72,128]{1,0:T(8,128)S(1)} collective-permute-done((f32[72,128]{1,0:T(8,128)S(1)}, f32[72,128]{1,0:T(8,128)S(1)}, u32[]{:S(2)}, u32[]{:S(2)}) %collective-permute-start.8) | collective-permute-done | bytes 36896 | tf_op jit(solution)/shard_map/ppermute | solution.py:534
  35.8 1.3 %shard_map.130 = f32[4,72,512]{2,1,0:T(8,128)} custom-call(f32[72,512]{1,0:T(8,128)S(1)} %get-tuple-element.21.refs_0_, f32[3,72,512]{2,1,0:T(8,128)S(1)} %get-tuple-element.20.refs_5_.refs_1_, f32[72,128]{1,0:T(8,128)S(1)} %get-tuple-element.22.refs_4_.refs_2_, f32[8,2432]{1,0:T(8,128)S(1)} %collective-permute-done.7.refs_8_.refs_3_, ...), custom_call_target="tpu_custom_call" | custom-call | tf_op jit(solution)/shard_map/pallas_call | solution.py:415
  (9 shorter events, 0.1 us)
Async XLA Ops:
  0.6 7.3 %copy-start.5 = (f32[14]{0:T(128)S(1)}, f32[14]{0:T(128)}, u32[]{:S(2)}) copy-start(f32[14]{0:T(128)} %param.21) | copy-start | bytes 172
  0.6 14.4 %copy-start.1 = (f32[72,512]{1,0:T(8,128)S(1)}, f32[72,512]{1,0:T(8,128)}, u32[]{:S(2)}) copy-start(f32[72,512]{1,0:T(8,128)} %refs_5_.1) | copy-start | bytes 442372
  3.0 5.0 %copy-start.4 = (f32[14,72]{1,0:T(8,128)S(1)}, f32[14,72]{1,0:T(8,128)}, u32[]{:S(2)}) copy-start(f32[14,72]{1,0:T(8,128)} %param.20) | copy-start | bytes 12100
  3.0 15.2 %collective-permute-start.3 = (f32[8,1280]{1,0:T(8,128)}, f32[8,1280]{1,0:T(8,128)S(1)}, u32[]{:S(2)}, u32[]{:S(2)}) collective-permute-start(f32[8,1280]{1,0:T(8,128)} %get-tuple-element.15), channel_id=1, source_target_pairs={{0,132},{1,68},{2,4},{3,196},{4,128},{5,64},{6,0},{7,192},{8,140},... | collective-permute-start | bytes 122888 | tf_op jit(solution)/shard_map/ppermute | solution.py:493
  5.7 12.5 %collective-permute-start.4 = (f32[8,1280]{1,0:T(8,128)}, f32[8,1280]{1,0:T(8,128)S(1)}, u32[]{:S(2)}, u32[]{:S(2)}) collective-permute-start(f32[8,1280]{1,0:T(8,128)} %get-tuple-element.16), channel_id=1, source_target_pairs={{0,164},{1,100},{2,36},{3,228},{4,160},{5,96},{6,32},{7,224},{8,17... | collective-permute-start | bytes 122888 | tf_op jit(solution)/shard_map/ppermute | solution.py:493
  7.9 7.1 %copy-start.3 = (f32[8,512]{1,0:T(8,128)S(1)}, f32[8,512]{1,0:T(8,128)}, u32[]{:S(2)}) copy-start(f32[8,512]{1,0:T(8,128)} %get-tuple-element.14.refs_0_.refs_6_) | copy-start | bytes 49156
  8.1 9.4 %collective-permute-start.2 = (f32[16,128]{1,0:T(8,128)S(1)}, f32[16,128]{1,0:T(8,128)S(1)}, u32[]{:S(2)}, u32[]{:S(2)}) collective-permute-start(f32[16,128]{1,0:T(8,128)S(1)} %select_maximum_fusion.refs_0_), channel_id=1, source_target_pairs={{0,7},{1,6},{2,5},{3,4},{4,3},{5,2},{6,1},{7,0},{8,15},{9,14},{10,... | collective-permute-start | bytes 24584 | tf_op jit(solution)/shard_map/ppermute | solution.py:494
  12.0 5.5 %collective-permute-start.1 = (f32[16,128]{1,0:T(8,128)S(1)}, f32[16,128]{1,0:T(8,128)S(1)}, u32[]{:S(2)}, u32[]{:S(2)}) collective-permute-start(f32[16,128]{1,0:T(8,128)S(1)} %select_maximum_fusion.refs_0_), channel_id=1, source_target_pairs={{0,6},{1,7},{2,4},{3,5},{4,2},{5,3},{6,0},{7,1},{8,14},{9,15},{10,... | collective-permute-start | bytes 24584 | tf_op jit(solution)/shard_map/ppermute | solution.py:494
  15.1 3.1 %collective-permute-start = (f32[16,128]{1,0:T(8,128)S(1)}, f32[16,128]{1,0:T(8,128)S(1)}, u32[]{:S(2)}, u32[]{:S(2)}) collective-permute-start(f32[16,128]{1,0:T(8,128)S(1)} %select_maximum_fusion.refs_0_), channel_id=1, source_target_pairs={{0,5},{1,4},{2,7},{3,6},{4,1},{5,0},{6,3},{7,2},{8,13},{9,12},{10,... | collective-permute-start | bytes 24584 | tf_op jit(solution)/shard_map/ppermute | solution.py:494
  15.1 1.0 %copy-start.2 = (f32[2,72,512]{2,1,0:T(8,128)S(1)}, f32[2,72,512]{2,1,0:T(8,128)}, u32[]{:S(2)}) copy-start(f32[2,72,512]{2,1,0:T(8,128)} %refs_2_.1) | copy-start | bytes 884740
  18.2 3.0 %copy-start = (f32[72,512]{1,0:T(8,128)S(1)}, f32[72,512]{1,0:T(8,128)}, u32[]{:S(2)}) copy-start(f32[72,512]{1,0:T(8,128)} %refs_0_.3) | copy-start | bytes 442372
  18.2 6.8 %collective-permute-start.5 = (f32[8,1280]{1,0:T(8,128)S(1)}, f32[8,1280]{1,0:T(8,128)S(1)}, u32[]{:S(2)}, u32[]{:S(2)}) collective-permute-start(f32[8,1280]{1,0:T(8,128)S(1)} %shard_map.124.refs_7_), channel_id=1, source_target_pairs={{0,20},{1,21},{2,22},{3,23},{4,16},{5,17},{6,18},{7,19},{8,28},{9,... | collective-permute-start | bytes 122888 | tf_op jit(solution)/shard_map/ppermute | solution.py:517
  25.0 3.5 %collective-permute-start.6 = (f32[8,1280]{1,0:T(8,128)S(1)}, f32[8,1280]{1,0:T(8,128)S(1)}, u32[]{:S(2)}, u32[]{:S(2)}) collective-permute-start(f32[8,1280]{1,0:T(8,128)S(1)} %shard_map.126.refs_7_), channel_id=1, source_target_pairs={{0,12},{1,13},{2,14},{3,15},{4,8},{5,9},{6,10},{7,11},{8,4},{9,5},... | collective-permute-start | bytes 122888 | tf_op jit(solution)/shard_map/ppermute | solution.py:526
  28.6 3.1 %collective-permute-start.7 = (f32[8,2432]{1,0:T(8,128)S(1)}, f32[8,2432]{1,0:T(8,128)S(1)}, u32[]{:S(2)}, u32[]{:S(2)}) collective-permute-start(f32[8,2432]{1,0:T(8,128)S(1)} %shard_map.128), channel_id=1, source_target_pairs={{0,4},{1,5},{2,6},{3,7},{4,0},{5,1},{6,2},{7,3},{8,12},{9,13},{10,... | collective-permute-start | bytes 233480 | tf_op jit(solution)/shard_map/ppermute | solution.py:536
  29.1 6.7 %collective-permute-start.8 = (f32[72,128]{1,0:T(8,128)S(1)}, f32[72,128]{1,0:T(8,128)S(1)}, u32[]{:S(2)}, u32[]{:S(2)}) collective-permute-start(f32[72,128]{1,0:T(8,128)S(1)} %get-tuple-element.22.refs_4_.refs_2_), channel_id=1, source_target_pairs={{0,252},{1,253},{2,254},{3,255},{4,8},{5,9},{6,10},{7,11},{8,4},{9... | collective-permute-start | bytes 110600 | tf_op jit(solution)/shard_map/ppermute | solution.py:534

commit v3 on v2

--- a/solution.py
+++ b/solution.py
@@ -17,6 +17,7 @@
 DIFFUSIVITY = 1.66
 SCALE = DIFFUSIVITY * math.log2(math.e)
 VMEM = pl.BlockSpec(memory_space=pltpu.VMEM)
+ANY = pl.BlockSpec(memory_space=pl.ANY)
 AXES = ("elem", "gpt")
 BF16 = jnp.bfloat16
 F32 = jnp.float32
@@ -62,17 +63,19 @@
 STRENGTH, LIT, ADJACENT, MU, ALBEDO = 0, 1, 2, 6, 7
 
 
-def pack_kernel(
-    t_ref, q_ref, mu_ref, albedo_ref, lit_ref, dest_ref, strength_ref, adjacent_ref,
-    low_ref, high_ref, scalar_ref,
-):
-    scalar_ref[STRENGTH : STRENGTH + 1] = strength_ref[...]
-    scalar_ref[LIT : LIT + 1] = lit_ref[...].astype(F32)
-    scalar_ref[ADJACENT:MU, :32] = adjacent_ref[...].astype(F32)
-    scalar_ref[MU : MU + 1] = mu_ref[...]
-    scalar_ref[ALBEDO : ALBEDO + 1] = albedo_ref[...]
+def pack_kernel(*refs):
+    sources, (low_ref, high_ref, scalar_ref), targets, sems = refs[:8], refs[8:11], refs[11:19], refs[19]
+    copies = [
+        pltpu.make_async_copy(source, target, sems.at[k])
+        for k, (source, target) in enumerate(zip(sources, targets))
+    ]
+    for copy in copies:
+        copy.start()
+    dest_ref, lit_ref, t_ref, q_ref, mu_ref, albedo_ref, strength_ref, adjacent_ref = targets
     served = (2 * (lax.axis_index("elem") >> 4) + 2 - lax.axis_index("gpt")) & 3
     before = jnp.where(iota((LANES, LANES), 0) < iota((LANES, LANES), 1), 1.0, 0.0).astype(BF16)
+    copies[0].wait()
+    copies[1].wait()
     dest = dest_ref[...]
     number_of = iota((64, LANES), 0)
     gone = jnp.zeros((64, 1), F32)
@@ -87,6 +90,13 @@
     apart = (dest ^ lax.axis_index("elem") ^ 1) & 15
     slot = jnp.where(sent, coded(apart) * 16 + rank, -1)
     chosen = jnp.where(slot == iota((256, COLS), 0), 1.0, 0.0).astype(BF16)
+    for copy in copies[2:]:
+        copy.wait()
+    scalar_ref[STRENGTH : STRENGTH + 1] = strength_ref[...]
+    scalar_ref[LIT : LIT + 1] = lit_ref[...].astype(F32)
+    scalar_ref[ADJACENT:MU, :32] = adjacent_ref[...].astype(F32)
+    scalar_ref[MU : MU + 1] = mu_ref[...]
+    scalar_ref[ALBEDO : ALBEDO + 1] = albedo_ref[...]
     row = iota((8, COLS), 0)
     tail = jnp.where(row == 0, mu_ref[...], jnp.where(row == 1, albedo_ref[...], 0.0))
     table = jnp.concatenate([t_ref[...] * q_ref[...], tail], axis=0)
@@ -139,7 +149,7 @@
         out_ref[:, WIDE + LANES * o : WIDE + LANES * o + LANES] = avg_ref[8 * o : 8 * o + 8]
 
 
-def heat_columns(a_ref, heat_ref, ext_ref, weight_ref, surface_ref, mu, albedo, tiles):
+def heat_columns(a_ref, heat_ref, ext_ref, weight_ref, surface_ref, parts_ref, mu, albedo, tiles):
     columns = a_ref.shape[1]
     slope = -1.0 / (DIFFUSIVITY * mu)
     total = jnp.dot(
@@ -164,12 +174,11 @@
                 flux = flux + (weight_ref[8 * o : 8 * o + 8] - surface_ref[8 * o : 8 * o + 8, at])
             start.append(flux)
 
-        def step(octet, carried, spans=spans, slopes=slopes):
+        def step(octet, carried, spans=spans, slopes=slopes, first=first):
             exts, depths, fluxes = carried
             depths, fluxes = [list(d) for d in depths], list(fluxes)
             base = pl.ds(pl.multiple_of(octet * 8, 8), 8)
             arrays = [a_ref[base, at] for at in spans]
-            heats = [[] for _ in spans]
             for s in range(8):
                 rows = [jnp.broadcast_to(a[s : s + 1], (8, LANES)) for a in arrays]
                 now = [None] * tiles
@@ -184,10 +193,9 @@
                         ] * jnp.exp2(depth)
                         now[t] = flux if now[t] is None else now[t] + flux
                 for t in range(tiles):
-                    heats[t].append(jnp.sum(fluxes[t] - now[t], axis=0, keepdims=True))
+                    at = pl.ds(pl.multiple_of(octet * 64 + 8 * s, 8), 8)
+                    parts_ref[first + t, at] = fluxes[t] - now[t]
                     fluxes[t] = now[t]
-            for t in range(tiles):
-                heat_ref[base, spans[t]] = jnp.concatenate(heats[t], axis=0)
             exts = [pltpu.roll(e, LANES - 8, 1) for e in exts]
             return exts, depths, fluxes
 
@@ -201,7 +209,13 @@
                 [[zero] * tiles for _ in range(GROUPS)],
                 start,
             ),
+            unroll=3,
         )
+    for tile in range(columns // LANES):
+        heat = parts_ref[tile, pl.ds(0, LEVELS, stride=8), :]
+        for s in range(1, 8):
+            heat = heat + parts_ref[tile, pl.ds(s, LEVELS, stride=8), :]
+        heat_ref[:, LANES * tile : LANES * tile + LANES] = heat
 
 
 def load_extinction(blocks, ext_ref):
@@ -232,7 +246,7 @@
             write(at, k)
         return carried
 
-    lax.fori_loop(0, LEVELS // 8, body, carried)
+    lax.fori_loop(0, LEVELS // 8, body, carried, unroll=3)
 
 
 def reader(ref, *first):
@@ -247,7 +261,7 @@
 
 
 def factor_kernel(
-    scalar_ref, q_ref, wind_ref,
+    scalar_ref, wind_ref,
     inv_ref, down_ref, ratio_ref, tend_ref,
     upper_ref, lower_ref, value_ref,
 ):
@@ -266,15 +280,15 @@
         return (ratio, values), (inverse, down, ratio, *values)
 
     zero = jnp.zeros((8, COLS), F32)
-    sides = [reader(q_ref), reader(wind_ref, 0), reader(wind_ref, 1)]
+    sides = [reader(wind_ref, 0), reader(wind_ref, 1)]
     sweep(
         (
             [reader(upper_ref), reader(lower_ref), *sides],
             [writer(inv_ref), writer(down_ref), writer(ratio_ref)]
-            + [writer(value_ref, f) for f in range(3)],
+            + [writer(value_ref, f) for f in range(2)],
         ),
         forward,
-        (zero, [zero] * 3),
+        (zero, [zero] * 2),
     )
 
     def backward(solved, ratio, *values):
@@ -283,52 +297,53 @@
 
     sweep(
         (
-            [reader(ratio_ref)] + [reader(value_ref, f) for f in range(3)],
-            [writer(value_ref, f) for f in range(3)],
+            [reader(ratio_ref)] + [reader(value_ref, f) for f in range(2)],
+            [writer(value_ref, f) for f in range(2)],
         ),
         backward,
-        [zero] * 3,
+        [zero] * 2,
         True,
     )
-    tend_ref[0] = value_ref[0] - q_ref[...]
-    tend_ref[1:3] = value_ref[1:3] - wind_ref[...]
+    tend_ref[...] = value_ref[...] - wind_ref[...]
 
 
 def home_kernel(
-    e0, e1, e2, e3, t_ref, q_ref, scalar_ref, out_ref, a_ref, ext_ref, weight_ref, surface_ref
+    e0, e1, e2, e3, t_ref, q_ref, scalar_ref, out_ref, a_ref, ext_ref, weight_ref, surface_ref, parts_ref
 ):
     load_extinction((e0, e1, e2, e3), ext_ref)
     a_ref[...] = t_ref[...] * q_ref[...]
     mu, albedo = scalar_ref[MU : MU + 1], scalar_ref[ALBEDO : ALBEDO + 1]
-    heat_columns(a_ref, out_ref, ext_ref, weight_ref, surface_ref, mu, albedo, 4)
+    heat_columns(a_ref, out_ref, ext_ref, weight_ref, surface_ref, parts_ref, mu, albedo, 4)
     out_ref[...] = out_ref[...] * scalar_ref[LIT : LIT + 1]
 
 
 def solve_kernel(
-    t_ref, flux_ref, inv_ref, down_ref, ratio_ref, late_ref, scalar_ref,
+    t_ref, q_ref, flux_ref, inv_ref, down_ref, ratio_ref, late_ref, scalar_ref,
     tend_ref, avg_ref, correct_ref,
-    heat_ref,
+    side_ref,
 ):
-    side = t_ref[...] + flux_ref[...]
-    heat_ref[...] = side * inv_ref[...]
-
-    def forward(value, side, down):
-        value = side + down * value
-        return value, (value,)
-
-    def backward(solved, value, ratio):
-        solved = value + ratio * solved
-        return solved, (solved,)
+    side_ref[0] = (t_ref[...] + flux_ref[...]) * inv_ref[...]
+    side_ref[1] = q_ref[...] * inv_ref[...]
+
+    def forward(values, down, *sides):
+        values = [side + down * value for side, value in zip(sides, values)]
+        return values, values
+
+    def backward(solved, ratio, *values):
+        solved = [value + ratio * x for value, x in zip(values, solved)]
+        return solved, solved
 
     zero = jnp.zeros((8, COLS), F32)
-    writes = [writer(heat_ref)]
-    sweep(([reader(heat_ref), reader(down_ref)], writes), forward, zero)
-    sweep(([reader(heat_ref), reader(ratio_ref)], writes), backward, zero, True)
-    tend = heat_ref[...] - t_ref[...]
-    tend_ref[...] = tend
-    avg = times(tend, element_mean(0))
-    for f in range(3):
-        avg = avg + times(late_ref[f], element_mean(f + 1))
+    sides = [reader(side_ref, f) for f in range(2)]
+    writes = [writer(side_ref, f) for f in range(2)]
+    sweep(([reader(down_ref), *sides], writes), forward, [zero] * 2)
+    sweep(([reader(ratio_ref), *sides], writes), backward, [zero] * 2, True)
+    tend_ref[0] = side_ref[0] - t_ref[...]
+    tend_ref[1] = side_ref[1] - q_ref[...]
+    avg = jnp.zeros((LEVELS, LANES), F32)
+    for f in range(2):
+        avg = avg + times(tend_ref[f], element_mean(f))
+        avg = avg + times(late_ref[f], element_mean(f + 2))
     avg_ref[...] = avg
     spread = jnp.where(iota((32, COLS), 0) == (iota((32, COLS), 1) >> 4), 1.0, 0.0).astype(BF16)
     row = iota((LANES, COLS), 0)
@@ -345,7 +360,7 @@
 
 def span_kernel(
     e0, e1, e2, e3, b0, b1, b2, b3, last_ref, out_ref, token_ref,
-    a_ref, heat_ref, ext_ref, weight_ref, surface_ref,
+    a_ref, heat_ref, ext_ref, weight_ref, surface_ref, parts_ref,
 ):
     load_extinction((e0, e1, e2, e3), ext_ref)
     place = lax.axis_index("elem") ^ 1
@@ -375,13 +390,14 @@
     albedo = a_ref[LEVELS + 1 : LEVELS + 2, :]
     occupied = mu > 0.0
     heat_columns(
-        a_ref, heat_ref, ext_ref, weight_ref, surface_ref, jnp.where(occupied, mu, 1.0), albedo, 2
+        a_ref, heat_ref, ext_ref, weight_ref, surface_ref, parts_ref,
+        jnp.where(occupied, mu, 1.0), albedo, 2,
     )
     out_ref[...] = jnp.where(occupied, heat_ref[...], 0.0)
     token_ref[...] = jnp.zeros_like(token_ref)
 
 
-def finish_kernel(tend0_ref, tend_ref, avg_ref, chip_ref, off_ref, correct_ref, out_ref):
+def finish_kernel(tend0_ref, tend_ref, avg_ref, chip_ref, off_ref, correct_ref, out_hbm, out_ref, sems):
     lane = iota((LEVELS, LANES), 1)
     first = (lax.axis_index("elem") & 1) == 0
     own, off = avg_ref[...], off_ref[...]
@@ -390,6 +406,7 @@
     )
     left, right = jnp.where(first, off, chip), jnp.where(first, chip, off)
     table = correct_ref[...]
+    copies = []
 
     def turned(x, by):
         by = by % LANES
@@ -402,11 +419,15 @@
             jnp.where(lane < 64, turned(own, 32 - 32 * f), turned(right, 64 - 32 * f)),
         )
         wide = jnp.where(lane < 96, wide, 0.0)
-        tend = tend0_ref[...] if f == 0 else tend_ref[f - 1]
+        tend = (tend0_ref if f < 2 else tend_ref)[f & 1]
         out_ref[f] = tend + times(wide, table)
-
-
-def call(kernel, outs, scratch, *args, limit=32, after=()):
+        copies.append(pltpu.make_async_copy(out_ref.at[f], out_hbm.at[f], sems.at[f]))
+        copies[f].start()
+    for copy in copies:
+        copy.wait()
+
+
+def call(kernel, outs, scratch, *args, limit=32, after=(), hbm_in=False, hbm_out=False):
     idle = len(after)
 
     def body(*refs):
@@ -415,8 +436,8 @@
     return pl.pallas_call(
         body,
         out_shape=outs,
-        in_specs=[VMEM] * len(args) + [pl.BlockSpec(memory_space=pl.ANY)] * idle,
-        out_specs=jax.tree.map(lambda _: VMEM, outs),
+        in_specs=[ANY if hbm_in else VMEM] * len(args) + [ANY] * idle,
+        out_specs=jax.tree.map(lambda _: ANY if hbm_out else VMEM, outs),
         scratch_shapes=scratch,
         compiler_params=pltpu.CompilerParams(vmem_limit_bytes=limit * 1024 * 1024),
     )(*args, *after)
@@ -476,33 +497,30 @@
         jnp.concatenate([optical_extinction, insolation_quadrature_share[:, None]], axis=1),
         ((0, 2), (0, LANES - LEVELS - 1)),
     )
+    params = (
+        row(destination_partition), lit, thermal_state, moisture_content,
+        mu, albedo, strength, adjacent_elements.T,
+    )
     low, high, scalars = call(
         pack_kernel,
         [message, message, shape(8, COLS)],
-        [],
-        thermal_state,
-        moisture_content,
-        mu,
-        albedo,
-        lit,
-        row(destination_partition),
-        strength,
-        adjacent_elements.T,
+        [pltpu.VMEM(x.shape, x.dtype) for x in params] + [pltpu.SemaphoreType.DMA((len(params),))],
+        *params,
         limit=60,
+        hbm_in=True,
     )
     blocks = [lax.ppermute(x, AXES, pairs) for x, pairs in zip((low, high), ACROSS)]
     exts = [own_ext] + [lax.ppermute(own_ext, AXES, pairs) for pairs in ASIDE]
     inverse, down, ratio, tend_late = call(
         factor_kernel,
         [
-            field, field, field, shape(3, LEVELS, COLS),
+            field, field, field, shape(2, LEVELS, COLS),
         ],
         [
             *[pltpu.VMEM((LEVELS, COLS), F32)] * 2,
-            pltpu.VMEM((3, LEVELS, COLS), F32),
+            pltpu.VMEM((2, LEVELS, COLS), F32),
         ],
         scalars,
-        moisture_content,
         lateral_velocity_components,
     )
 
@@ -511,6 +529,7 @@
             pltpu.VMEM((56, LANES), F32),
             pltpu.VMEM((56, LANES), F32),
             pltpu.VMEM((56, columns), F32),
+            pltpu.VMEM((columns // LANES, 8 * LEVELS, LANES), F32),
         ]
 
     sent = call(next_kernel, message, [], *blocks, after=(ratio, *exts[1:]))
@@ -526,9 +545,9 @@
     blocks.append(lax.ppermute(sent, AXES, SWAPS[1]))
     tend0, average, correct = call(
         solve_kernel,
-        [field, shape(LEVELS, LANES), shape(LANES, COLS, dtype=BF16)],
-        [pltpu.VMEM((LEVELS, COLS), F32)],
-        thermal_state, heat, inverse, down, ratio, tend_late, scalars,
+        [shape(2, LEVELS, COLS), shape(LEVELS, LANES), shape(LANES, COLS, dtype=BF16)],
+        [pltpu.VMEM((2, LEVELS, COLS), F32)],
+        thermal_state, moisture_content, heat, inverse, down, ratio, tend_late, scalars,
         after=(sent,),
     )
     off = lax.ppermute(average, AXES, OFF_CHIP)
@@ -541,9 +560,11 @@
         *exts, *blocks, last,
     )
     tendency_out = call(
-        finish_kernel, shape(4, LEVELS, COLS), [],
+        finish_kernel, shape(4, LEVELS, COLS),
+        [pltpu.VMEM((4, LEVELS, COLS), F32), pltpu.SemaphoreType.DMA((4,))],
         tend0, tend_late, average, last, off, correct,
         after=(token,),
+        hbm_out=True,
     )
     return tendency_out, span_heating
 

time: 37.3 us -> 37 us (level)
  waiting for transfers between devices: 3.31 us -> 4.42 us
  local copies, waits for them, and re-layouts: 1.07 us -> 0.12 us
  Pallas kernels: 13.2 us -> 12.6 us
    ppermute x3, waiting for transfers between devices: 0.63 us -> 1.98 us  [shards(): exts = [own_ext] + [lax.ppermute(own_ext, AXES, pairs) for pairs in ASIDE]]
    unnamed x12, local copies, waits for them, and re-layouts: 0.98 us -> 0.03 us
    pallas_call x9, Pallas kernels: 13.2 us -> 12.6 us  [call(): pl.pallas_call(body, out_shape=outs, in_specs=[ANY if hbm_in else VMEM] *...]
  transfers between devices with their start and end apart: 9 -> 9, of which waited for: 3 -> 4; matrix products, arithmetic and copies ran while one was open for 0% -> 0% of each run, Pallas kernels for 26% -> 25%
where the time goes in v3:
time: 37 us; the launch traced here: 36.8 us
  starting transfers between devices  18.9 us (51%)
  Pallas kernels  12.6 us (34%)
  waiting for transfers between devices  4.42 us (12%)
  between operations  0.74 us (2%)
    pallas_call x9, Pallas kernels, call(): pl.pallas_call(body, out_shape=outs, in_specs=[ANY if hbm_in else VMEM] *...  12.6 us
    ppermute x3, starting transfers between devices, shards(): exts = [own_ext] + [lax.ppermute(own_ext, AXES, pairs) for pairs in ASIDE]  6.94 us
    ppermute x2, starting transfers between devices, shards(): lax.ppermute(x, AXES, pairs)  4.97 us
    ppermute x1, starting transfers between devices, shards(): blocks.append(lax.ppermute(sent, AXES, SWAPS[2]))  3 us
    ppermute x1, starting transfers between devices, shards(): off = lax.ppermute(average, AXES, OFF_CHIP)  2.66 us
    ppermute x3, waiting for transfers between devices, shards(): exts = [own_ext] + [lax.ppermute(own_ext, AXES, pairs) for pairs in ASIDE]  1.98 us
    ppermute x1, waiting for transfers between devices, shards(): blocks.append(lax.ppermute(sent, AXES, SWAPS[1]))  1.6 us
    ppermute x1, waiting for transfers between devices, shards(): off = lax.ppermute(average, AXES, OFF_CHIP)  0.82 us
  transfers between devices with their start and end apart: 9, of which 4 were waited for; matrix products, arithmetic and copies ran while one was open for 0% of the time, Pallas kernels for 25%

profile of v3, /device:TPU:2, one launch (start us, length us, event | category | flops | bytes accessed | tf_op | source)
XLA Modules:
  0.0 36.8 jit_solution(6722082185364587479)
XLA Ops:
  0.6 0.0 copy-start.2
  0.6 0.0 copy-start.5
  0.7 2.3 %shard_map.122 = (f32[8,1280]{1,0:T(8,128)}, f32[8,1280]{1,0:T(8,128)}, f32[8,512]{1,0:T(8,128)}) custom-call(s32[1,512]{1,0:T(1,128)} %bitcast.7, s32[1,512]{1,0:T(1,128)} %bitcast.8, f32[72,512]{1,0:T(8,128)} %refs_0_.1, f32[72,512]{1,0:T(8,128)} %refs_1_.3, f32[1,512]{1,0:T(1,128)} %bitcast.9, f32[1,512]{1,0:T(1,128)} %bitcast.10, f32[1,512]{1,0:T(1,128)} %bitcast.11, ...), custom_call_target="tpu_custom_call" | custom-call | tf_op jit(solution)/shard_map/pallas_call | solution.py:436
  2.9 0.0 copy-start.4
  2.9 2.8 %collective-permute-start.3 = (f32[8,1280]{1,0:T(8,128)}, f32[8,1280]{1,0:T(8,128)S(1)}, u32[]{:S(2)}, u32[]{:S(2)}) collective-permute-start(f32[8,1280]{1,0:T(8,128)} %get-tuple-element.15), channel_id=1, source_target_pairs={{0,132},{1,68},{2,4},{3,196},{4,128},{5,64},{6,0},{7,192},{8,140},... | collective-permute-start | bytes 122888 | tf_op jit(solution)/shard_map/ppermute | solution.py:512
  5.7 2.2 %collective-permute-start.4 = (f32[8,1280]{1,0:T(8,128)}, f32[8,1280]{1,0:T(8,128)S(1)}, u32[]{:S(2)}, u32[]{:S(2)}) collective-permute-start(f32[8,1280]{1,0:T(8,128)} %get-tuple-element.16), channel_id=1, source_target_pairs={{0,164},{1,100},{2,36},{3,228},{4,160},{5,96},{6,32},{7,224},{8,17... | collective-permute-start | bytes 122888 | tf_op jit(solution)/shard_map/ppermute | solution.py:512
  7.9 0.1 copy.13
  8.0 0.0 copy-done.4
  8.0 0.1 select_maximum_fusion.refs_0_
  8.1 3.9 %collective-permute-start.2 = (f32[16,128]{1,0:T(8,128)S(1)}, f32[16,128]{1,0:T(8,128)S(1)}, u32[]{:S(2)}, u32[]{:S(2)}) collective-permute-start(f32[16,128]{1,0:T(8,128)S(1)} %select_maximum_fusion.refs_0_), channel_id=1, source_target_pairs={{0,7},{1,6},{2,5},{3,4},{4,3},{5,2},{6,1},{7,0},{8,15},{9,14},{10,... | collective-permute-start | bytes 24584 | tf_op jit(solution)/shard_map/ppermute | solution.py:513
  12.0 3.0 %collective-permute-start.1 = (f32[16,128]{1,0:T(8,128)S(1)}, f32[16,128]{1,0:T(8,128)S(1)}, u32[]{:S(2)}, u32[]{:S(2)}) collective-permute-start(f32[16,128]{1,0:T(8,128)S(1)} %select_maximum_fusion.refs_0_), channel_id=1, source_target_pairs={{0,6},{1,7},{2,4},{3,5},{4,2},{5,3},{6,0},{7,1},{8,14},{9,15},{10,... | collective-permute-start | bytes 24584 | tf_op jit(solution)/shard_map/ppermute | solution.py:513
  15.0 0.0 collective-permute-start
  15.0 0.0 copy-done.3
  15.0 1.1 %shard_map.123 = (f32[72,512]{1,0:T(8,128)S(1)}, f32[72,512]{1,0:T(8,128)S(1)}, f32[72,512]{1,0:T(8,128)S(1)}, f32[2,72,512]{2,1,0:T(8,128)S(1)}) custom-call(f32[8,512]{1,0:T(8,128)S(1)} %copy-done.3, f32[2,72,512]{2,1,0:T(8,128)S(1)} %copy-done.2), custom_call_target="tpu_custom_call" | custom-call | tf_op jit(solution)/shard_map/pallas_call | solution.py:436
  16.2 0.0 collective-permute-done.2.refs_5_.refs_3_
  16.2 0.4 %collective-permute-done.1.refs_4_.refs_2_ = f32[16,128]{1,0:T(8,128)S(1)} collective-permute-done((f32[16,128]{1,0:T(8,128)S(1)}, f32[16,128]{1,0:T(8,128)S(1)}, u32[]{:S(2)}, u32[]{:S(2)}) %collective-permute-start.1) | collective-permute-done | bytes 8224 | tf_op jit(solution)/shard_map/ppermute | solution.py:513
  16.6 1.6 %collective-permute-done.refs_3_.refs_1_ = f32[16,128]{1,0:T(8,128)S(1)} collective-permute-done((f32[16,128]{1,0:T(8,128)S(1)}, f32[16,128]{1,0:T(8,128)S(1)}, u32[]{:S(2)}, u32[]{:S(2)}) %collective-permute-start) | collective-permute-done | bytes 8224 | tf_op jit(solution)/shard_map/ppermute | solution.py:513
  18.2 0.0 collective-permute-done.3.refs_0_.refs_4_
  18.2 0.0 collective-permute-done.4.refs_1_.refs_5_
  18.2 0.0 copy-start.1
  18.2 3.0 %collective-permute-start.5 = (f32[8,1280]{1,0:T(8,128)S(1)}, f32[8,1280]{1,0:T(8,128)S(1)}, u32[]{:S(2)}, u32[]{:S(2)}) collective-permute-start(f32[8,1280]{1,0:T(8,128)S(1)} %shard_map.124.refs_7_), channel_id=1, source_target_pairs={{0,20},{1,21},{2,22},{3,23},{4,16},{5,17},{6,18},{7,19},{8,28},{9,... | collective-permute-start | bytes 122888 | tf_op jit(solution)/shard_map/ppermute | solution.py:536
  21.2 3.6 %shard_map.125.refs_3_.refs_2_ = f32[72,512]{1,0:T(8,128)S(1)} custom-call(f32[16,128]{1,0:T(8,128)S(1)} %select_maximum_fusion.refs_0_, f32[16,128]{1,0:T(8,128)S(1)} %collective-permute-done.refs_3_.refs_1_, f32[16,128]{1,0:T(8,128)S(1)} %collective-permute-done.1.refs_4_.refs_2_, f32[16,128]{1,0:T(8,128)S(1)} %collective-permute-done.2.refs_5_.refs_3_, ...), custom_call_target="tpu_custom_call" | custom-call | tf_op jit(solution)/shard_map/pallas_call | solution.py:436
  24.8 0.0 collective-permute-done.5.refs_2_.refs_6_
  24.9 0.8 %collective-permute-start.6 = (f32[8,1280]{1,0:T(8,128)S(1)}, f32[8,1280]{1,0:T(8,128)S(1)}, u32[]{:S(2)}, u32[]{:S(2)}) collective-permute-start(f32[8,1280]{1,0:T(8,128)S(1)} %shard_map.126.refs_8_), channel_id=1, source_target_pairs={{0,12},{1,13},{2,14},{3,15},{4,8},{5,9},{6,10},{7,11},{8,4},{9,5},... | collective-permute-start | bytes 122888 | tf_op jit(solution)/shard_map/ppermute | solution.py:545
  25.6 1.1 %shard_map.127 = (f32[2,72,512]{2,1,0:T(8,128)S(1)}, f32[72,128]{1,0:T(8,128)S(1)}, bf16[128,512]{1,0:T(8,128)(2,1)S(1)}) custom-call(f32[72,512]{1,0:T(8,128)S(1)} %copy-done, f32[72,512]{1,0:T(8,128)S(1)} %copy-done.1, f32[72,512]{1,0:T(8,128)S(1)} %shard_map.125.refs_3_.refs_2_, f32[72,512]{1,0:T(8,128)S(1)} %get-tuple-element.18.refs_3_, ...), custom_call_target="tpu_custom_call" | custom-call | tf_op jit(solution)/shard_map/pallas_call | solution.py:436
  26.8 1.6 %collective-permute-done.6.refs_3_.refs_7_ = f32[8,1280]{1,0:T(8,128)S(1)} collective-permute-done((f32[8,1280]{1,0:T(8,128)S(1)}, f32[8,1280]{1,0:T(8,128)S(1)}, u32[]{:S(2)}, u32[]{:S(2)}) %collective-permute-start.6) | collective-permute-done | bytes 40992 | tf_op jit(solution)/shard_map/ppermute | solution.py:545
  28.4 0.5 %collective-permute-start.7 = (f32[8,2432]{1,0:T(8,128)S(1)}, f32[8,2432]{1,0:T(8,128)S(1)}, u32[]{:S(2)}, u32[]{:S(2)}) collective-permute-start(f32[8,2432]{1,0:T(8,128)S(1)} %shard_map.128), channel_id=1, source_target_pairs={{0,4},{1,5},{2,6},{3,7},{4,0},{5,1},{6,2},{7,3},{8,12},{9,13},{10,... | collective-permute-start | bytes 233480 | tf_op jit(solution)/shard_map/ppermute | solution.py:555
  28.9 2.7 %collective-permute-start.8 = (f32[72,128]{1,0:T(8,128)S(1)}, f32[72,128]{1,0:T(8,128)S(1)}, u32[]{:S(2)}, u32[]{:S(2)}) collective-permute-start(f32[72,128]{1,0:T(8,128)S(1)} %get-tuple-element.22.refs_4_.refs_2_), channel_id=1, source_target_pairs={{0,252},{1,253},{2,254},{3,255},{4,8},{5,9},{6,10},{7,11},{8,4},{9... | collective-permute-start | bytes 110600 | tf_op jit(solution)/shard_map/ppermute | solution.py:553
  31.6 0.0 collective-permute-done.7.refs_8_.refs_3_
  31.6 3.2 %shard_map.129 = (f32[72,256]{1,0:T(8,128)}, f32[8,128]{1,0:T(8,128)S(1)}) custom-call(f32[16,128]{1,0:T(8,128)S(1)} %select_maximum_fusion.refs_0_, f32[16,128]{1,0:T(8,128)S(1)} %collective-permute-done.refs_3_.refs_1_, f32[16,128]{1,0:T(8,128)S(1)} %collective-permute-done.1.refs_4_.refs_2_, f32[16,128]{1,0:T(8,128)S(1)} %collective-permute-done.2.refs_5_.refs_3_, ...), custom_call_target="tpu_custom_call" | custom-call | tf_op jit(solution)/shard_map/pallas_call | solution.py:436
  34.8 0.8 %collective-permute-done.8.refs_4_ = f32[72,128]{1,0:T(8,128)S(1)} collective-permute-done((f32[72,128]{1,0:T(8,128)S(1)}, f32[72,128]{1,0:T(8,128)S(1)}, u32[]{:S(2)}, u32[]{:S(2)}) %collective-permute-start.8) | collective-permute-done | bytes 36896 | tf_op jit(solution)/shard_map/ppermute | solution.py:553
  35.6 1.2 %shard_map.130 = f32[4,72,512]{2,1,0:T(8,128)} custom-call(f32[2,72,512]{2,1,0:T(8,128)S(1)} %get-tuple-element.21.refs_0_, f32[2,72,512]{2,1,0:T(8,128)S(1)} %get-tuple-element.20.refs_6_.refs_1_, f32[72,128]{1,0:T(8,128)S(1)} %get-tuple-element.22.refs_4_.refs_2_, f32[8,2432]{1,0:T(8,128)S(1)} %collective-permute-done.7.refs_8_.refs_3_, ...), custom_call_target="tpu_custom_call" | custom-call | tf_op jit(solution)/shard_map/pallas_call | solution.py:436
  (9 shorter events, 0.1 us)
Async XLA Ops:
  0.6 14.4 %copy-start.2 = (f32[2,72,512]{2,1,0:T(8,128)S(1)}, f32[2,72,512]{2,1,0:T(8,128)}, u32[]{:S(2)}) copy-start(f32[2,72,512]{2,1,0:T(8,128)} %refs_1_.2) | copy-start | bytes 884740
  0.6 7.3 %copy-start.5 = (f32[14]{0:T(128)S(1)}, f32[14]{0:T(128)}, u32[]{:S(2)}) copy-start(f32[14]{0:T(128)} %param.21) | copy-start | bytes 172
  2.9 5.1 %copy-start.4 = (f32[14,72]{1,0:T(8,128)S(1)}, f32[14,72]{1,0:T(8,128)}, u32[]{:S(2)}) copy-start(f32[14,72]{1,0:T(8,128)} %param.20) | copy-start | bytes 12100
  2.9 15.2 %collective-permute-start.3 = (f32[8,1280]{1,0:T(8,128)}, f32[8,1280]{1,0:T(8,128)S(1)}, u32[]{:S(2)}, u32[]{:S(2)}) collective-permute-start(f32[8,1280]{1,0:T(8,128)} %get-tuple-element.15), channel_id=1, source_target_pairs={{0,132},{1,68},{2,4},{3,196},{4,128},{5,64},{6,0},{7,192},{8,140},... | collective-permute-start | bytes 122888 | tf_op jit(solution)/shard_map/ppermute | solution.py:512
  5.7 12.5 %collective-permute-start.4 = (f32[8,1280]{1,0:T(8,128)}, f32[8,1280]{1,0:T(8,128)S(1)}, u32[]{:S(2)}, u32[]{:S(2)}) collective-permute-start(f32[8,1280]{1,0:T(8,128)} %get-tuple-element.16), channel_id=1, source_target_pairs={{0,164},{1,100},{2,36},{3,228},{4,160},{5,96},{6,32},{7,224},{8,17... | collective-permute-start | bytes 122888 | tf_op jit(solution)/shard_map/ppermute | solution.py:512
  7.9 7.1 %copy-start.3 = (f32[8,512]{1,0:T(8,128)S(1)}, f32[8,512]{1,0:T(8,128)}, u32[]{:S(2)}) copy-start(f32[8,512]{1,0:T(8,128)} %get-tuple-element.14.refs_0_.refs_6_.refs_7_) | copy-start | bytes 49156
  8.1 8.1 %collective-permute-start.2 = (f32[16,128]{1,0:T(8,128)S(1)}, f32[16,128]{1,0:T(8,128)S(1)}, u32[]{:S(2)}, u32[]{:S(2)}) collective-permute-start(f32[16,128]{1,0:T(8,128)S(1)} %select_maximum_fusion.refs_0_), channel_id=1, source_target_pairs={{0,7},{1,6},{2,5},{3,4},{4,3},{5,2},{6,1},{7,0},{8,15},{9,14},{10,... | collective-permute-start | bytes 24584 | tf_op jit(solution)/shard_map/ppermute | solution.py:513
  12.0 4.6 %collective-permute-start.1 = (f32[16,128]{1,0:T(8,128)S(1)}, f32[16,128]{1,0:T(8,128)S(1)}, u32[]{:S(2)}, u32[]{:S(2)}) collective-permute-start(f32[16,128]{1,0:T(8,128)S(1)} %select_maximum_fusion.refs_0_), channel_id=1, source_target_pairs={{0,6},{1,7},{2,4},{3,5},{4,2},{5,3},{6,0},{7,1},{8,14},{9,15},{10,... | collective-permute-start | bytes 24584 | tf_op jit(solution)/shard_map/ppermute | solution.py:513
  15.0 3.1 %collective-permute-start = (f32[16,128]{1,0:T(8,128)S(1)}, f32[16,128]{1,0:T(8,128)S(1)}, u32[]{:S(2)}, u32[]{:S(2)}) collective-permute-start(f32[16,128]{1,0:T(8,128)S(1)} %select_maximum_fusion.refs_0_), channel_id=1, source_target_pairs={{0,5},{1,4},{2,7},{3,6},{4,1},{5,0},{6,3},{7,2},{8,13},{9,12},{10,... | collective-permute-start | bytes 24584 | tf_op jit(solution)/shard_map/ppermute | solution.py:513
  18.2 3.0 %copy-start = (f32[72,512]{1,0:T(8,128)S(1)}, f32[72,512]{1,0:T(8,128)}, u32[]{:S(2)}) copy-start(f32[72,512]{1,0:T(8,128)} %refs_0_.1) | copy-start | bytes 442372
  18.2 3.0 %copy-start.1 = (f32[72,512]{1,0:T(8,128)S(1)}, f32[72,512]{1,0:T(8,128)}, u32[]{:S(2)}) copy-start(f32[72,512]{1,0:T(8,128)} %refs_1_.3) | copy-start | bytes 442372
  18.2 6.6 %collective-permute-start.5 = (f32[8,1280]{1,0:T(8,128)S(1)}, f32[8,1280]{1,0:T(8,128)S(1)}, u32[]{:S(2)}, u32[]{:S(2)}) collective-permute-start(f32[8,1280]{1,0:T(8,128)S(1)} %shard_map.124.refs_7_), channel_id=1, source_target_pairs={{0,20},{1,21},{2,22},{3,23},{4,16},{5,17},{6,18},{7,19},{8,28},{9,... | collective-permute-start | bytes 122888 | tf_op jit(solution)/shard_map/ppermute | solution.py:536
  24.9 3.5 %collective-permute-start.6 = (f32[8,1280]{1,0:T(8,128)S(1)}, f32[8,1280]{1,0:T(8,128)S(1)}, u32[]{:S(2)}, u32[]{:S(2)}) collective-permute-start(f32[8,1280]{1,0:T(8,128)S(1)} %shard_map.126.refs_8_), channel_id=1, source_target_pairs={{0,12},{1,13},{2,14},{3,15},{4,8},{5,9},{6,10},{7,11},{8,4},{9,5},... | collective-permute-start | bytes 122888 | tf_op jit(solution)/shard_map/ppermute | solution.py:545
  28.4 3.2 %collective-permute-start.7 = (f32[8,2432]{1,0:T(8,128)S(1)}, f32[8,2432]{1,0:T(8,128)S(1)}, u32[]{:S(2)}, u32[]{:S(2)}) collective-permute-start(f32[8,2432]{1,0:T(8,128)S(1)} %shard_map.128), channel_id=1, source_target_pairs={{0,4},{1,5},{2,6},{3,7},{4,0},{5,1},{6,2},{7,3},{8,12},{9,13},{10,... | collective-permute-start | bytes 233480 | tf_op jit(solution)/shard_map/ppermute | solution.py:555
  28.9 6.7 %collective-permute-start.8 = (f32[72,128]{1,0:T(8,128)S(1)}, f32[72,128]{1,0:T(8,128)S(1)}, u32[]{:S(2)}, u32[]{:S(2)}) collective-permute-start(f32[72,128]{1,0:T(8,128)S(1)} %get-tuple-element.22.refs_4_.refs_2_), channel_id=1, source_target_pairs={{0,252},{1,253},{2,254},{3,255},{4,8},{5,9},{6,10},{7,11},{8,4},{9... | collective-permute-start | bytes 110600 | tf_op jit(solution)/shard_map/ppermute | solution.py:553
